TPU v7x, 32 devices: a whole 2x2x4 slice. The times are simulated.
32 devices in a mesh: inst: 8 (over z, y), tp: 4 (over x, core).
Axes of the slice: x: 2, y: 2, z: 4, core: 2. Of those that a mesh axis runs over, the one named last changes fastest.
Arguments:
- ssm_state: bfloat16 [112, 128, 64, 128], P('inst', 'tp'), may hold values from -6 to 6
- conv_x: bfloat16 [112, 3, 8192], P('inst', None, 'tp'), may hold values from -6 to 6
- conv_bc: bfloat16 [112, 3, 1024], P('inst', None, 'tp'), may hold values from -6 to 6
- k_cache: bfloat16 [112, 64, 1024], P('inst', None, 'tp'), may hold values from -5 to 5
- v_cache: bfloat16 [112, 64, 1024], P('inst', None, 'tp'), may hold values from -5 to 5
- context_len: int32 [112], P('inst'), may hold values from 1 to 61, as said below
- dest_inst: int32 [112], P('inst'), may hold values from 0 to 7, as said below
- dest_slot: int32 [112], P('inst'), may hold values from 0 to 13, as said below
- x_in: bfloat16 [3, 112, 8192], P(None, 'inst', 'tp'), may hold values from -6 to 6
- bc_in: bfloat16 [3, 112, 1024], P(None, 'inst', 'tp'), may hold values from -6 to 6
- z_in: bfloat16 [3, 112, 8192], P(None, 'inst', 'tp'), may hold values from -6 to 6
- dt_in: float32 [3, 112, 128], P(None, 'inst', 'tp'), may hold values from -4 to 4
- q_in: bfloat16 [3, 112, 4096], P(None, 'inst', 'tp'), may hold values from -100 to 100
- k_in: bfloat16 [3, 112, 1024], P(None, 'inst', 'tp'), may hold values from -5 to 5
- v_in: bfloat16 [3, 112, 1024], P(None, 'inst', 'tp'), may hold values from -5 to 5
- conv_wx: float32 [4, 8192], P(None, 'tp'), may hold values from -3 to 3
- conv_wbc: float32 [4, 1024], P(None, 'tp'), may hold values from -3 to 3
- a_rate: float32 [128], P('tp'), may hold values from 0.02 to 3
- dt_bias: float32 [128], P('tp'), may hold values from -1 to 1
- d_skip: float32 [128], P('tp'), may hold values from 1 to 4
- norm_gain: bfloat16 [8192], P('tp'), may hold values from 0.5 to 1.5
- o_proj: bfloat16 [4096, 4096], P('tp'), may hold values from -0.09375 to 0.09375
Outputs:
- ssm_final: bfloat16 [112, 128, 64, 128], P('inst', 'tp')
- convx_final: bfloat16 [112, 3, 8192], P('inst', None, 'tp')
- convbc_final: bfloat16 [112, 3, 1024], P('inst', None, 'tp')
- k_final: bfloat16 [112, 64, 1024], P('inst', None, 'tp')
- v_final: bfloat16 [112, 64, 1024], P('inst', None, 'tp')
- mamba_out: bfloat16 [3, 112, 8192], P(None, 'inst', 'tp')
- attn_out: bfloat16 [3, 112, 4096], P(None, 'inst', 'tp')
Inputs may be any that keep to these rules, and one draw needn't show every extreme that they name: Row r's request moves to row dest_inst * 14 + dest_slot; this map is a permutation of all rows. A request that stays keeps its slot. At every instance exactly one request stays, 13 leave and 13 arrive; an instance sends at most 2 requests to any other instance, and every instance sends exactly 2 to some other. `dest_slot`: see dest_inst. `context_len`: some row has exactly 61, some exactly 1.
All inputs are finite; a program needn't handle non-finite values.
Results may differ from a plain program's by a relative error of at most 0.011.
Values may be sent and summed in bfloat16 or wider, within the bound.
A program may use at most 192 MiB of HBM per device.

v0:
```python
import jax
import jax.numpy as jnp
from jax import lax
from jax.sharding import PartitionSpec as P

STEPS = 3
QHEADS = 32
KVHEADS = 8
HEAD_DIM = 128


def pack_rows(onehot, source_item):
    flat = source_item.reshape(source_item.shape[0], -1)
    moved = jnp.dot(onehot, flat, preferred_element_type=jnp.float32)
    return moved.astype(source_item.dtype).reshape((onehot.shape[0],) + source_item.shape[1:])


def place_rows(take, received, own_item, staying):
    incoming = pack_rows(take, received)
    keep = staying.reshape((-1,) + (1,) * (own_item.ndim - 1))
    return jnp.where(keep, own_item, incoming)


def on_device(
    ssm_state,
    conv_x,
    conv_bc,
    k_cache,
    v_cache,
    context_len,
    dest_inst,
    dest_slot,
    x_in,
    bc_in,
    z_in,
    dt_in,
    q_in,
    k_in,
    v_in,
    conv_wx,
    conv_wbc,
    a_rate,
    dt_bias,
    d_skip,
    norm_gain,
    o_proj,
):
    peer_count = lax.axis_size("inst")
    my_index = lax.axis_index("inst")
    slot_count = context_len.shape[0]
    per_peer = (slot_count - 2) // (peer_count - 1) + 1
    staying = dest_inst == my_index
    leaving = jnp.logical_not(staying)
    slot_ids = jnp.arange(slot_count, dtype=jnp.int32)
    earlier = (
        (dest_inst[None, :] == dest_inst[:, None])
        & leaving[None, :]
        & (slot_ids[None, :] < slot_ids[:, None])
    )
    rank_here = jnp.sum(earlier.astype(jnp.int32), axis=1)
    bucket = dest_inst * per_peer + rank_here
    bucket_ids = jnp.arange(peer_count * per_peer, dtype=jnp.int32)
    chosen = (bucket[None, :] == bucket_ids[:, None]) & leaving[None, :]
    chosen_int = chosen.astype(jnp.int32)
    onehot = chosen.astype(jnp.bfloat16)
    plan_rows = jnp.stack(
        [
            jnp.sum(chosen_int * dest_slot[None, :], axis=1),
            jnp.sum(chosen_int, axis=1),
            jnp.sum(chosen_int * context_len[None, :], axis=1),
        ],
        axis=1,
    )
    arrived = lax.all_to_all(plan_rows, "inst", split_axis=0, concat_axis=0, tiled=True)
    take_bool = (arrived[None, :, 1] == 1) & (arrived[None, :, 0] == slot_ids[:, None])
    take_int = take_bool.astype(jnp.int32)
    take = take_bool.astype(jnp.bfloat16)
    live_len = jnp.where(staying, context_len, jnp.sum(take_int * arrived[None, :, 2], axis=1))
    out_state = pack_rows(onehot, ssm_state)
    out_convx = pack_rows(onehot, conv_x)
    out_convbc = pack_rows(onehot, conv_bc)
    out_keys = pack_rows(onehot, k_cache)
    out_values = pack_rows(onehot, v_cache)
    got_state, got_convx, got_convbc, got_keys, got_values = (
        lax.all_to_all(out_state, "inst", split_axis=0, concat_axis=0, tiled=True),
        lax.all_to_all(out_convx, "inst", split_axis=0, concat_axis=0, tiled=True),
        lax.all_to_all(out_convbc, "inst", split_axis=0, concat_axis=0, tiled=True),
        lax.all_to_all(out_keys, "inst", split_axis=0, concat_axis=0, tiled=True),
        lax.all_to_all(out_values, "inst", split_axis=0, concat_axis=0, tiled=True),
    )
    state_now = place_rows(take, got_state, ssm_state, staying)
    window_x = place_rows(take, got_convx, conv_x, staying)
    window_bc = place_rows(take, got_convbc, conv_bc, staying)
    key_rows = place_rows(take, got_keys, k_cache, staying)
    value_rows = place_rows(take, got_values, v_cache, staying)
    head_count = ssm_state.shape[1]
    head_size = ssm_state.shape[2]
    state_size = ssm_state.shape[3]
    group_count = conv_bc.shape[2] // (2 * state_size)
    kv_count = k_cache.shape[2] // HEAD_DIM
    query_group = QHEADS // KVHEADS
    cache_len = k_cache.shape[1]
    score_scale = 1.0 / HEAD_DIM**0.5
    positions = jnp.arange(cache_len, dtype=jnp.int32)
    mamba_list = []
    attn_list = []
    for decode_step in range(STEPS):
        full_x = jnp.concatenate([window_x, x_in[decode_step][:, None, :]], axis=1)
        conv_out_x = jax.nn.silu(jnp.sum(full_x.astype(jnp.float32) * conv_wx[None], axis=1))
        window_x = full_x[:, 1:]
        full_bc = jnp.concatenate([window_bc, bc_in[decode_step][:, None, :]], axis=1)
        conv_out_bc = jax.nn.silu(jnp.sum(full_bc.astype(jnp.float32) * conv_wbc[None], axis=1))
        window_bc = full_bc[:, 1:]
        xs_heads = conv_out_x.reshape(slot_count, head_count, head_size)
        pairs = conv_out_bc.reshape(slot_count, group_count, 2, state_size)
        b_heads = jnp.repeat(pairs[:, :, 0], head_count // group_count, axis=1)
        c_heads = jnp.repeat(pairs[:, :, 1], head_count // group_count, axis=1)
        delta = jax.nn.softplus(dt_in[decode_step] + dt_bias[None])
        decay = jnp.exp(-delta * a_rate[None])
        fresh = (
            state_now.astype(jnp.float32) * decay[:, :, None, None]
            + (delta[:, :, None] * xs_heads)[:, :, :, None] * b_heads[:, :, None, :]
        )
        y_heads = jnp.sum(fresh * c_heads[:, :, None, :], axis=3) + d_skip[None, :, None] * xs_heads
        state_now = fresh.astype(jnp.bfloat16)
        gated = y_heads.reshape(slot_count, -1) * jax.nn.silu(z_in[decode_step].astype(jnp.float32))
        grouped = gated.reshape(slot_count, group_count, -1)
        normed = grouped * lax.rsqrt(jnp.mean(grouped * grouped, axis=2, keepdims=True) + 1e-05)
        mamba_list.append(
            (normed.reshape(slot_count, -1) * norm_gain.astype(jnp.float32)[None]).astype(
                jnp.bfloat16
            )
        )
        write_pos = live_len + decode_step
        written = positions[None, :, None] == write_pos[:, None, None]
        key_rows = jnp.where(written, k_in[decode_step][:, None, :], key_rows)
        value_rows = jnp.where(written, v_in[decode_step][:, None, :], value_rows)
        queries = q_in[decode_step].reshape(slot_count, kv_count, query_group, HEAD_DIM)
        key_heads = key_rows.reshape(slot_count, cache_len, kv_count, HEAD_DIM)
        value_heads = value_rows.reshape(slot_count, cache_len, kv_count, HEAD_DIM)
        scores = (
            jnp.einsum("skgd,sckd->skgc", queries, key_heads, preferred_element_type=jnp.float32)
            * score_scale
        )
        visible = positions[None, None, None, :] <= write_pos[:, None, None, None]
        scores = jnp.where(visible, scores, -jnp.inf)
        top_score = jnp.max(scores, axis=3, keepdims=True)
        raised = jnp.exp(scores - top_score)
        weights = (raised / jnp.sum(raised, axis=3, keepdims=True)).astype(jnp.bfloat16)
        mixed = jnp.einsum(
            "skgc,sckd->skgd", weights, value_heads, preferred_element_type=jnp.float32
        ).astype(jnp.bfloat16)
        mixed = mixed.reshape(slot_count, -1)
        partial_value = jnp.dot(mixed, o_proj, preferred_element_type=jnp.float32)
        attn_list.append(
            lax.psum_scatter(
                partial_value.astype(jnp.bfloat16), "tp", scatter_dimension=1, tiled=True
            )
        )
    attn_all = jnp.stack(attn_list)
    return (state_now, window_x, window_bc, key_rows, value_rows, jnp.stack(mamba_list), attn_all)


def solution(mesh):
    in_specs = (
        P("inst", "tp", None, None),
        P("inst", None, "tp"),
        P("inst", None, "tp"),
        P("inst", None, "tp"),
        P("inst", None, "tp"),
        P("inst"),
        P("inst"),
        P("inst"),
        P(None, "inst", "tp"),
        P(None, "inst", "tp"),
        P(None, "inst", "tp"),
        P(None, "inst", "tp"),
        P(None, "inst", "tp"),
        P(None, "inst", "tp"),
        P(None, "inst", "tp"),
        P(None, "tp"),
        P(None, "tp"),
        P("tp"),
        P("tp"),
        P("tp"),
        P("tp"),
        P("tp", None),
    )
    out_specs = (
        P("inst", "tp", None, None),
        P("inst", None, "tp"),
        P("inst", None, "tp"),
        P("inst", None, "tp"),
        P("inst", None, "tp"),
        P(None, "inst", "tp"),
        P(None, "inst", "tp"),
    )
    return jax.shard_map(
        on_device, mesh=mesh, in_specs=in_specs, out_specs=out_specs, check_vma=False
    )
```

profile of v0, /device:TPU:0, one launch (start us, length us, event | category | flops | bytes accessed | tf_op | source)
XLA Modules:
  0.0 365.1 jit_solution(6815655282666070451)
XLA Ops:
  11.3 7.3 %all-to-all-start = ((s32[8,2,3]{2,1,0:T(2,128)}), s32[8,2,3]{2,1,0:T(2,128)S(1)}, u32[]{:S(2)}, u32[]{:S(2)}) async-start(s32[8,2,3]{2,1,0:T(2,128)} %copy.90), calls=%async_computation | async-start | bytes 16384 | tf_op jit(solution)/shard_map/all_to_all | solution.py:74
  20.1 1.1 copy.93
  21.5 3.6 all-to-all-done
  25.1 3.3 all-to-all-start.3
  29.6 5.5 %all-to-all-done.3 = bf16[16,3,256]{2,1,0:T(4,128)(2,1)S(1)} async-done(((bf16[16,3,256]{2,1,0:T(4,128)(2,1)}), bf16[16,3,256]{2,1,0:T(4,128)(2,1)S(1)}, u32[]{:S(2)}, u32[]{:S(2)}) %all-to-all-start.3) | async-done | bytes 24608 | tf_op jit(solution)/shard_map/all_to_all | solution.py:87
  35.1 3.4 all-to-all-start.2
  41.0 5.6 %all-to-all-done.2 = bf16[16,3,2048]{2,1,0:T(4,128)(2,1)S(1)} async-done(((bf16[16,3,2048]{2,1,0:T(4,128)(2,1)}), bf16[16,3,2048]{2,1,0:T(4,128)(2,1)S(1)}, u32[]{:S(2)}, u32[]{:S(2)}) %all-to-all-start.2) | async-done | bytes 196640 | tf_op jit(solution)/shard_map/all_to_all | solution.py:86
  46.6 3.5 all-to-all-start.5
  51.7 9.4 %all-to-all-done.5 = bf16[16,64,256]{2,1,0:T(8,128)(2,1)S(1)} async-done(((bf16[16,64,256]{2,1,0:T(8,128)(2,1)}), bf16[16,64,256]{2,1,0:T(8,128)(2,1)S(1)}, u32[]{:S(2)}, u32[]{:S(2)}) %all-to-all-start.5) | async-done | bytes 524320 | tf_op jit(solution)/shard_map/all_to_all | solution.py:89
  61.1 3.7 %all-to-all-start.4 = ((bf16[16,64,256]{2,1,0:T(8,128)(2,1)}), bf16[16,64,256]{2,1,0:T(8,128)(2,1)S(1)}, u32[]{:S(2)}, u32[]{:S(2)}) async-start(bf16[16,64,256]{2,1,0:T(8,128)(2,1)} %bitcast.77), calls=%async_computation.4 | async-start | bytes 1048576 | tf_op jit(solution)/shard_map/all_to_all | solution.py:88
  64.8 7.1 %pad.21 = bf16[16,2048,128]{2,1,0:T(8,128)(2,1)} pad(bf16[14,2048,128]{2,1,0:T(8,128)(2,1)} %bitcast.297, bf16[]{:T(256)} %constant.69), padding=0_2x0_0x0_0 | pad | bytes 15728642
  71.9 8.2 %copy.126 = bf16[2,8,2048,128]{3,1,2,0:T(8,128)(2,1)S(1)} copy(bf16[2,8,2048,128]{3,2,1,0:T(8,128)(2,1)} %bitcast.294) | data formatting | bytes 16777216
  80.1 5.5 %fusion.8 = bf16[2,8,2048,128]{3,1,2,0:T(8,128)(2,1)} fusion(bf16[14,262144]{1,0:T(8,128)(2,1)S(1)} %bitcast.293, s32[14]{0:T(128)S(1)} %multiply_add_fusion.3, pred[14]{0:T(512)(128)(4,1)S(1)} %get-tuple-element.63), kind=kOutput, calls=%fused_computation.26 | convolution fusion | flops 121635264 | bytes 15728710 | tf_op jit(solution)/shard_map/dot_general | solution.py:14
  85.6 8.1 %copy.127 = bf16[2,8,2048,128]{3,2,1,0:T(8,128)(2,1)} copy(bf16[2,8,2048,128]{3,1,2,0:T(8,128)(2,1)} %fusion.8) | data formatting | bytes 16777216
  93.9 6.1 %all-to-all-start.1 = ((bf16[16,32,64,128]{3,2,1,0:T(8,128)(2,1)}), bf16[16,32,64,128]{3,2,1,0:T(8,128)(2,1)}, u32[]{:S(2)}, u32[]{:S(2)}) async-start(bf16[16,32,64,128]{3,2,1,0:T(8,128)(2,1)} %bitcast.295), calls=%async_computation.1 | async-start | bytes 16777216 | tf_op jit(solution)/shard_map/all_to_all | solution.py:85
  111.9 1.4 multiply_reduce_fusion.5
  118.3 2.0 fusion.36
  122.2 1.3 fusion.16
  124.1 1.4 convolution_convert_fusion.11
  125.5 5.3 %convolution_convert_fusion.8 = bf16[14,4096]{1,0:T(8,128)(2,1)} fusion(bf16[14,1024]{1,0:T(8,128)(2,1)S(1)} %reshape.990, bf16[1024,4096]{1,0:T(8,128)(2,1)} %param.43), kind=kOutput, calls=%fused_computation.23 | convolution fusion | flops 117497856 | bytes 8531968 | tf_op jit(solution)/shard_map/dot_general | solution.py:154
  132.6 5.2 %convolution_convert_fusion.9 = bf16[14,4096]{1,0:T(8,128)(2,1)} fusion(bf16[14,1024]{1,0:T(8,128)(2,1)S(1)} %reshape.987, bf16[1024,4096]{1,0:T(8,128)(2,1)} %param.43), kind=kOutput, calls=%fused_computation.24 | convolution fusion | flops 117497856 | bytes 8531968 | tf_op jit(solution)/shard_map/dot_general | solution.py:154
  138.6 5.3 %convolution_convert_fusion.10 = bf16[14,4096]{1,0:T(8,128)(2,1)} fusion(bf16[14,1024]{1,0:T(8,128)(2,1)S(1)} %reshape.984, bf16[1024,4096]{1,0:T(8,128)(2,1)} %param.43), kind=kOutput, calls=%fused_computation.25 | convolution fusion | flops 117497856 | bytes 8531968 | tf_op jit(solution)/shard_map/dot_general | solution.py:154
  144.0 7.7 %reduce-scatter.8.cloned.1.call-done = bf16[14,1024]{1,0:T(8,128)(2,1)} async-done(((bf16[14,4096]{1,0:T(8,128)(2,1)}), bf16[14,1024]{1,0:T(8,128)(2,1)}) %reduce-scatter.8.cloned.1.call-update) | async-done | bytes 28688 | tf_op jit(solution)/shard_map/reduce_scatter | solution.py:156
  151.7 22.8 %reduce-scatter.6.cloned.1.call-done = bf16[14,1024]{1,0:T(8,128)(2,1)} async-done(((bf16[14,4096]{1,0:T(8,128)(2,1)}), bf16[14,1024]{1,0:T(8,128)(2,1)}) %reduce-scatter.6.cloned.1.call-update) | async-done | bytes 28688 | tf_op jit(solution)/shard_map/reduce_scatter | solution.py:156
  174.5 22.1 %reduce-scatter.4.cloned.1.call-done = bf16[14,1024]{1,0:T(8,128)(2,1)} async-done(((bf16[14,4096]{1,0:T(8,128)(2,1)}), bf16[14,1024]{1,0:T(8,128)(2,1)}) %reduce-scatter.4.cloned.1.call-update) | async-done | bytes 28688 | tf_op jit(solution)/shard_map/reduce_scatter | solution.py:156
  196.6 1.4 pad_maximum_fusion.4
  198.0 82.5 %all-to-all-done.1 = bf16[16,32,64,128]{3,2,1,0:T(8,128)(2,1)} async-done(((bf16[16,32,64,128]{3,2,1,0:T(8,128)(2,1)}), bf16[16,32,64,128]{3,2,1,0:T(8,128)(2,1)}, u32[]{:S(2)}, u32[]{:S(2)}) %all-to-all-start.1) | async-done | bytes 8388640 | tf_op jit(solution)/shard_map/all_to_all | solution.py:85
  280.5 11.5 %convolution_convert_fusion = bf16[14,262144]{1,0:T(8,128)(2,1)} fusion(bf16[2,8,2048,128]{3,2,1,0:T(8,128)(2,1)} %bitcast.57, s32[16]{0:T(128)S(1)} %bitcast.336, pred[16]{0:T(512)(128)(4,1)S(1)} %bitcast.342), kind=kOutput, calls=%fused_computation.3 | convolution fusion | flops 121110976 | bytes 15728720 | tf_op jit(solution)/shard_map/dot_general | solution.py:14
  292.1 8.1 %copy.129 = bf16[2,8,2048,128]{3,2,1,0:T(8,128)(2,1)} copy(bf16[2,8,2048,128]{3,1,2,0:T(8,128)(2,1)} %bitcast.292) | data formatting | bytes 16777216
  300.2 6.9 %slice.165 = bf16[14,2048,128]{2,1,0:T(8,128)(2,1)} slice(bf16[16,2048,128]{2,1,0:T(8,128)(2,1)} %bitcast.296), slice={[0:14], [0:2048], [0:128]} | slice | bytes 14680064
  307.2 31.8 %multiply_reduce_fusion.1 = (f32[14,32,64]{2,1,0:T(8,128)S(1)}, f32[14,32,64]{2,1,0:T(8,128)S(1)}, f32[14,32,64]{2,1,0:T(8,128)S(1)}, bf16[14,32,64,128]{3,2,1,0:T(8,128)(2,1)}) fusion(f32[14,128]{1,0:T(8,128)S(1)} %copy-done.20, f32[14,128]{1,0:T(8,128)S(1)} %copy-done.15, f32[14,32,64]{2,1,0:T(8,128)S(1)} %get-tuple-element.106, ...), kind=kLoop, calls=%fused_computation.10 | loop fusion | flops 76984320 | bytes 22756622 | tf_op jit(solution)/shard_map/reduce_sum | solution.py:124
  339.7 17.4 %fusion.3 = bf16[14,32,64,128]{3,2,1,0:T(8,128)(2,1)} fusion(f32[14,128]{1,0:T(8,128)S(1)} %copy-done.14, f32[14,32,64]{2,1,0:T(8,128)S(1)} %get-tuple-element.105, f32[14,32]{1,0:T(8,128)S(1)} %get-tuple-element.76, f32[14,128]{1,0:T(8,128)S(1)} %copy-done.15, f32[14,32,64]{2,1,0:T(8,128)S(1)} %get-tuple-element.106, f32[14,32]{1,0:T(8,128)S(1)} %get-tuple-element.74, ...), kind=kLoop, calls=%fused_computation.13 | loop fusion | flops 55050240 | bytes 15051008 | tf_op jit(solution)/shard_map/convert_element_type | solution.py:125
  (215 shorter events, 34.8 us)
Async XLA Ops:
  7.2 43.0 %copy-start.1 = (bf16[14,64,256]{2,1,0:T(8,128)(2,1)S(1)}, bf16[14,64,256]{2,1,0:T(8,128)(2,1)}, u32[]{:S(2)}) copy-start(bf16[14,64,256]{2,1,0:T(8,128)(2,1)} %param.25) | copy-start | bytes 1376260
  7.9 103.1 %copy-start.32 = (pred[14]{0:T(512)(128)(4,1)}, pred[14]{0:T(512)(128)(4,1)S(1)}, u32[]{:S(2)}) copy-start(pred[14]{0:T(512)(128)(4,1)S(1)} %get-tuple-element.64) | copy-start | bytes 46
  11.3 13.8 %all-to-all-start = ((s32[8,2,3]{2,1,0:T(2,128)}), s32[8,2,3]{2,1,0:T(2,128)S(1)}, u32[]{:S(2)}, u32[]{:S(2)}) async-start(s32[8,2,3]{2,1,0:T(2,128)} %copy.90), calls=%async_computation | async-start | bytes 16384 | tf_op jit(solution)/shard_map/all_to_all | solution.py:74
  25.1 10.0 %all-to-all-start.3 = ((bf16[16,3,256]{2,1,0:T(4,128)(2,1)}), bf16[16,3,256]{2,1,0:T(4,128)(2,1)S(1)}, u32[]{:S(2)}, u32[]{:S(2)}) async-start(bf16[16,3,256]{2,1,0:T(4,128)(2,1)} %reshape.971), calls=%async_computation.3 | async-start | bytes 65536 | tf_op jit(solution)/shard_map/all_to_all | solution.py:87
  35.1 11.6 %all-to-all-start.2 = ((bf16[16,3,2048]{2,1,0:T(4,128)(2,1)}), bf16[16,3,2048]{2,1,0:T(4,128)(2,1)S(1)}, u32[]{:S(2)}, u32[]{:S(2)}) async-start(bf16[16,3,2048]{2,1,0:T(4,128)(2,1)} %reshape.967), calls=%async_computation.2 | async-start | bytes 524288 | tf_op jit(solution)/shard_map/all_to_all | solution.py:86
  46.6 14.5 %all-to-all-start.5 = ((bf16[16,64,256]{2,1,0:T(8,128)(2,1)}), bf16[16,64,256]{2,1,0:T(8,128)(2,1)S(1)}, u32[]{:S(2)}, u32[]{:S(2)}) async-start(bf16[16,64,256]{2,1,0:T(8,128)(2,1)} %bitcast.87), calls=%async_computation.5 | async-start | bytes 1048576 | tf_op jit(solution)/shard_map/all_to_all | solution.py:89
  61.1 32.6 %all-to-all-start.4 = ((bf16[16,64,256]{2,1,0:T(8,128)(2,1)}), bf16[16,64,256]{2,1,0:T(8,128)(2,1)S(1)}, u32[]{:S(2)}, u32[]{:S(2)}) async-start(bf16[16,64,256]{2,1,0:T(8,128)(2,1)} %bitcast.77), calls=%async_computation.4 | async-start | bytes 1048576 | tf_op jit(solution)/shard_map/all_to_all | solution.py:88
  93.7 7.5 %copy-start.41 = (f32[32]{0:T(128)S(1)}, f32[32]{0:T(128)}, u32[]{:S(2)}) copy-start(f32[32]{0:T(128)} %param.41) | copy-start | bytes 388
  93.8 7.7 %copy-start.11 = (bf16[3,14,1024]{2,1,0:T(8,128)(2,1)S(1)}, bf16[3,14,1024]{2,1,0:T(8,128)(2,1)}, u32[]{:S(2)}) copy-start(bf16[3,14,1024]{2,1,0:T(8,128)(2,1)} %param.34) | copy-start | bytes 258052
  93.8 9.6 %copy-start.29 = (f32[3,14,32]{2,1,0:T(8,128)S(1)}, f32[3,14,32]{2,1,0:T(8,128)}, u32[]{:S(2)}) copy-start(f32[3,14,32]{2,1,0:T(8,128)} %param.33) | copy-start | bytes 16132
  93.8 9.5 %copy-start.39 = (f32[32]{0:T(128)S(1)}, f32[32]{0:T(128)}, u32[]{:S(2)}) copy-start(f32[32]{0:T(128)} %param.39) | copy-start | bytes 388
  93.8 9.5 %copy-start.40 = (f32[32]{0:T(128)S(1)}, f32[32]{0:T(128)}, u32[]{:S(2)}) copy-start(f32[32]{0:T(128)} %param.40) | copy-start | bytes 388
  93.8 10.2 %copy-start.30 = (bf16[3,14,256]{2,1,0:T(8,128)(2,1)S(1)}, bf16[3,14,256]{2,1,0:T(8,128)(2,1)}, u32[]{:S(2)}) copy-start(bf16[3,14,256]{2,1,0:T(8,128)(2,1)} %param.36) | copy-start | bytes 64516
  93.8 10.2 %copy-start.31 = (bf16[3,14,256]{2,1,0:T(8,128)(2,1)S(1)}, bf16[3,14,256]{2,1,0:T(8,128)(2,1)}, u32[]{:S(2)}) copy-start(bf16[3,14,256]{2,1,0:T(8,128)(2,1)} %param.35) | copy-start | bytes 64516
  93.8 11.3 %copy-start.36 = (s32[14]{0:T(128)S(1)}, s32[14]{0:T(128)}, u32[]{:S(2)}) copy-start(s32[14]{0:T(128)} %param.27) | copy-start | bytes 172
  93.8 12.8 %copy-start.12 = (bf16[14,3,256]{2,0,1:T(8,128)(2,1)S(1)}, bf16[14,3,256]{2,0,1:T(8,128)(2,1)}, u32[]{:S(2)}) copy-start(bf16[14,3,256]{2,0,1:T(8,128)(2,1)} %param.24) | copy-start | bytes 64516
  93.8 13.0 %copy-start.35 = (f32[4,256]{1,0:T(4,128)S(1)}, f32[4,256]{1,0:T(4,128)}, u32[]{:S(2)}) copy-start(f32[4,256]{1,0:T(4,128)} %param.38) | copy-start | bytes 12292
  93.9 17.1 %copy-start.5 = (bf16[14,3,2048]{2,0,1:T(8,128)(2,1)S(1)}, bf16[14,3,2048]{2,0,1:T(8,128)(2,1)}, u32[]{:S(2)}) copy-start(bf16[14,3,2048]{2,0,1:T(8,128)(2,1)} %param.23) | copy-start | bytes 516100
  93.9 18.0 %copy-start.21 = (f32[4,2048]{1,0:T(4,128)S(1)}, f32[4,2048]{1,0:T(4,128)}, u32[]{:S(2)}) copy-start(f32[4,2048]{1,0:T(4,128)} %param.37) | copy-start | bytes 98308
  93.9 186.7 %all-to-all-start.1 = ((bf16[16,32,64,128]{3,2,1,0:T(8,128)(2,1)}), bf16[16,32,64,128]{3,2,1,0:T(8,128)(2,1)}, u32[]{:S(2)}, u32[]{:S(2)}) async-start(bf16[16,32,64,128]{3,2,1,0:T(8,128)(2,1)} %bitcast.295), calls=%async_computation.1 | async-start | bytes 16777216 | tf_op jit(solution)/shard_map/all_to_all | solution.py:85
  100.0 18.3 %copy-start = (bf16[14,64,256]{2,1,0:T(8,128)(2,1)S(1)}, bf16[14,64,256]{2,1,0:T(8,128)(2,1)}, u32[]{:S(2)}) copy-start(bf16[14,64,256]{2,1,0:T(8,128)(2,1)} %param.26) | copy-start | bytes 1376260
  100.0 51.7 %reduce-scatter.8.cloned.1.call-start = ((), (), s32[]{:S(2)}) async-start(), calls=%async_computation.11 | async-start | bytes 163840 | tf_op jit(solution)/shard_map/reduce_scatter | solution.py:156
  122.1 8.7 %copy-start.7 = (bf16[14,64,256]{2,1,0:T(8,128)(2,1)}, bf16[14,64,256]{2,1,0:T(8,128)(2,1)S(1)}, u32[]{:S(2)}) copy-start(bf16[14,64,256]{2,1,0:T(8,128)(2,1)S(1)} %get-tuple-element.98) | copy-start | bytes 1376260
  122.1 8.7 %copy-start.9 = (bf16[14,8,2,8,128]{4,3,2,1,0:T(8,128)(2,1)S(1)}, bf16[14,8,2,8,128]{4,3,2,1,0:T(8,128)(2,1)}, u32[]{:S(2)}) copy-start(bf16[14,8,2,8,128]{4,3,2,1,0:T(8,128)(2,1)} %get-tuple-element.95) | copy-start | bytes 1376260
  122.1 8.7 %copy-start.23 = (bf16[14,2,4,128]{3,2,1,0:T(4,128)(2,1)S(1)}, bf16[14,2,4,128]{3,2,1,0:T(4,128)(2,1)}, u32[]{:S(2)}) copy-start(bf16[14,2,4,128]{3,2,1,0:T(4,128)(2,1)} %reshape_squeeze.10) | copy-start | bytes 86020
  122.2 8.7 %copy-start.38 = (pred[14,64]{1,0:T(8,128)(4,1)S(1)}, pred[14,64]{1,0:T(8,128)(4,1)}, u32[]{:S(2)}) copy-start(pred[14,64]{1,0:T(8,128)(4,1)} %get-tuple-element.101) | copy-start | bytes 2692
  130.8 43.7 %reduce-scatter.6.cloned.1.call-start = ((), (), s32[]{:S(2)}) async-start(), calls=%async_computation.10 | async-start | bytes 163840 | tf_op jit(solution)/shard_map/reduce_scatter | solution.py:156
  137.8 142.7 %copy-start.25 = (s32[16,1]{0,1:T(1,128)S(1)}, s32[16,1]{0,1:T(1,128)}, u32[]{:S(2)}) copy-start(s32[16,1]{0,1:T(1,128)} %copy-done.24) | copy-start | bytes 196
  137.8 142.7 %copy-start.27 = (pred[16,1]{0,1:T(4,128)(4,1)S(1)}, pred[16,1]{0,1:T(4,128)(4,1)}, u32[]{:S(2)}) copy-start(pred[16,1]{0,1:T(4,128)(4,1)} %copy-done.26) | copy-start | bytes 52
  138.3 58.2 %reduce-scatter.4.cloned.1.call-start = ((), (), s32[]{:S(2)}) async-start(), calls=%async_computation.9 | async-start | bytes 163840 | tf_op jit(solution)/shard_map/reduce_scatter | solution.py:156
  339.3 17.9 %copy-start.4 = (bf16[3,14,2048]{2,1,0:T(8,128)(2,1)S(1)}, bf16[3,14,2048]{2,1,0:T(8,128)(2,1)}, u32[]{:S(2)}) copy-start(bf16[3,14,2048]{2,1,0:T(8,128)(2,1)} %param.32) | copy-start | bytes 516100
  339.6 17.9 %copy-start.17 = (f32[2048]{0:T(1024)S(1)}, f32[2048]{0:T(1024)}, u32[]{:S(2)}) copy-start(f32[2048]{0:T(1024)} %convert_element_type.194) | copy-start | bytes 24580
  (22 other events, 133.8 us)
Sparse Core Ops, SparseCore 0:
  130.9 20.7 reduce-scatter.7
  154.9 19.5 reduce-scatter.5
  176.9 19.5 reduce-scatter.3
where the time goes:
time: 366 us; the launch traced here: 365 us
  waiting for transfers between devices  159 us (43%)
  other arithmetic  65.6 us (18%)
  local copies, waits for them, and re-layouts  57.4 us (16%)
  matrix products  40.2 us (11%)
  starting transfers between devices  27.9 us (8%)
  between operations  14.7 us (4%)
    all_to_all x1, waiting for transfers between devices, on_device(): lax.all_to_all(out_state, 'inst', split_axis=0, concat_axis=0, tiled=True)  82.5 us
    reduce_scatter x3, waiting for transfers between devices, on_device(): lax.psum_scatter(partial_value.astype(jnp.bfloat16), 'tp', scatter_dimens...  52.5 us
    unnamed x122, local copies, waits for them, and re-layouts  50.4 us
    reduce_sum x1, other arithmetic, on_device(): jnp.sum(fresh * c_heads[:, :, None, :], axis=3)  31.8 us
    dot_general x10, matrix products, pack_rows(): moved = jnp.dot(onehot, flat, preferred_element_type=jnp.float32)  20.2 us
    convert_element_type x1, other arithmetic, on_device(): state_now = fresh.astype(jnp.bfloat16)  17.4 us
    dot_general x3, matrix products, on_device(): partial_value = jnp.dot(mixed, o_proj, preferred_element_type=jnp.float32)  15.8 us
    all_to_all x1, waiting for transfers between devices, on_device(): lax.all_to_all(out_values, 'inst', split_axis=0, concat_axis=0, tiled=True)  9.39 us
  transfers between devices with their start and end apart: 9, of which 8 were waited for; matrix products, arithmetic and copies ran while one was open for 22% of the time, Pallas kernels for 0%

commit v1 on v0

v1 whole, which is shorter than its diff:
```python
import functools

import jax
import jax.numpy as jnp
from jax import lax
from jax.experimental import pallas as pl
from jax.experimental.pallas import tpu as pltpu
from jax.sharding import PartitionSpec as P

STEPS = 3
QHEADS = 32
KVHEADS = 8
HEAD_DIM = 128
CHUNKS = (24, 8)


def pack_small_kernel(src_ref, row_ref, k_ref, v_ref, extra_ref, out_ref):
    cache_len = k_ref.shape[1]
    for b in range(out_ref.shape[0]):
        out_ref[b, :cache_len] = k_ref[src_ref[b]]
        out_ref[b, cache_len : 2 * cache_len] = v_ref[src_ref[b]]
        out_ref[b, 2 * cache_len :] = extra_ref[row_ref[b]]


def pack_state_kernel(buckets, src_ref, state_ref, *rest):
    outs, sems = rest[: len(CHUNKS)], rest[len(CHUNKS)]
    copies = []
    at = 0
    for c, heads in enumerate(CHUNKS):
        for b in range(buckets):
            copies.append(
                pltpu.make_async_copy(
                    state_ref.at[src_ref[b], pl.ds(at, heads)], outs[c].at[b], sems.at[c, b]
                )
            )
        at += heads
    for copy in copies:
        copy.start()
    for copy in copies:
        copy.wait()


def unpack_kernel(take_ref, got_ref, k_ref, v_ref, extra_ref):
    cache_len = k_ref.shape[1]
    for s in range(k_ref.shape[0]):
        k_ref[s] = got_ref[take_ref[s], :cache_len]
        v_ref[s] = got_ref[take_ref[s], cache_len : 2 * cache_len]
        extra_ref[s] = got_ref[take_ref[s], 2 * cache_len :]


def state_kernel(first, head_count, take_ref, carry_ref, got_ref, u_ref, b_ref, c_ref, *rest):
    final_ref, y_ref = rest[-2:]
    slot = pl.program_id(0)
    heads, size, width = got_ref.shape[1:]
    old = got_ref[0].reshape(heads * size, width)
    both = lax.dot_general(
        c_ref[0], old, (((1,), (1,)), ((), ())), preferred_element_type=jnp.float32
    )
    y_ref[0] = both[:8] + both[8:]
    added = lax.dot_general(
        u_ref[0], b_ref[0], (((0,), (0,)), ((), ())), preferred_element_type=jnp.float32
    )
    for h in range(heads):
        kept = got_ref[0, h].astype(jnp.float32) * carry_ref[slot * head_count + first + h]
        final_ref[0, h] = (kept + added[h * size : (h + 1) * size]).astype(jnp.bfloat16)


def split_two(value):
    high = lax.reduce_precision(value, 8, 7)
    return high.astype(jnp.bfloat16), (value - high).astype(jnp.bfloat16)


def on_device(
    ssm_state,
    conv_x,
    conv_bc,
    k_cache,
    v_cache,
    context_len,
    dest_inst,
    dest_slot,
    x_in,
    bc_in,
    z_in,
    dt_in,
    q_in,
    k_in,
    v_in,
    conv_wx,
    conv_wbc,
    a_rate,
    dt_bias,
    d_skip,
    norm_gain,
    o_proj,
):
    bf16, f32 = jnp.bfloat16, jnp.float32
    peer_count = lax.axis_size("inst")
    slot_count = context_len.shape[0]
    per_peer = (slot_count - 2) // (peer_count - 1) + 1
    buckets = peer_count * per_peer
    head_count, head_size, state_size = ssm_state.shape[1:]
    cache_len, kv_width = k_cache.shape[1:]
    channels = head_count * head_size
    anywhere = pl.BlockSpec(memory_space=pl.ANY)
    in_vmem = pl.BlockSpec(memory_space=pltpu.VMEM)
    in_smem = pl.BlockSpec(memory_space=pltpu.SMEM)

    slot_ids = jnp.arange(slot_count, dtype=jnp.int32)
    earlier = (dest_inst[None, :] == dest_inst[:, None]) & (slot_ids[None, :] < slot_ids[:, None])
    rank_here = jnp.sum(earlier.astype(jnp.int32), axis=1)
    bucket = dest_inst * per_peer + rank_here
    bucket_ids = jnp.arange(buckets, dtype=jnp.int32)
    chosen = bucket[None, :] == bucket_ids[:, None]
    row = jnp.min(jnp.where(chosen, slot_ids[None, :], slot_count), axis=1)
    src = jnp.where(row == slot_count, 0, row)

    x_rows = 3 * channels // kv_width
    bc_rows = 3 * conv_bc.shape[2] // kv_width
    used = x_rows + bc_rows
    extra_rows = -(-(used + 1) // 16) * 16
    plan = jnp.stack([dest_slot, context_len], axis=1).astype(bf16)
    plan = jnp.pad(plan, ((0, 1), (0, 0)), constant_values=-1)
    plan = jnp.pad(plan, ((0, 0), (0, kv_width - 2)))[:, None, :]
    extra = jnp.concatenate(
        [
            conv_x.reshape(slot_count, x_rows, kv_width),
            conv_bc.reshape(slot_count, bc_rows, kv_width),
        ],
        axis=1,
    )
    extra = jnp.concatenate([jnp.pad(extra, ((0, 1), (0, 0), (0, 0))), plan], axis=1)
    extra = jnp.pad(extra, ((0, 0), (0, extra_rows - used - 1), (0, 0)))
    small_rows = 2 * cache_len + extra_rows
    small = pl.pallas_call(
        pack_small_kernel,
        out_shape=jax.ShapeDtypeStruct((buckets, small_rows, kv_width), bf16),
        in_specs=[in_smem, in_smem, in_vmem, in_vmem, in_vmem],
        out_specs=in_vmem,
        cost_estimate=pl.CostEstimate(flops=0, bytes_accessed=4000000, transcendentals=0),
        compiler_params=pltpu.CompilerParams(vmem_limit_bytes=32 * 1024 * 1024),
    )(src, row, k_cache, v_cache, extra)
    packed = pl.pallas_call(
        functools.partial(pack_state_kernel, buckets),
        out_shape=[
            jax.ShapeDtypeStruct((buckets, heads, head_size, state_size), bf16) for heads in CHUNKS
        ],
        in_specs=[in_smem, anywhere],
        out_specs=[anywhere] * len(CHUNKS),
        scratch_shapes=[pltpu.SemaphoreType.DMA((len(CHUNKS), buckets))],
        cost_estimate=pl.CostEstimate(
            flops=0, bytes_accessed=4 * ssm_state.size, transcendentals=0
        ),
    )(src, ssm_state)

    got_small = lax.all_to_all(small, "inst", split_axis=0, concat_axis=0, tiled=True)
    got_state = [
        lax.all_to_all(part, "inst", split_axis=0, concat_axis=0, tiled=True) for part in packed
    ]

    arrived = got_small[:, 2 * cache_len + used, :2].astype(jnp.int32)
    hit = arrived[None, :, 0] == slot_ids[:, None]
    take = jnp.max(jnp.where(hit, bucket_ids[None, :], 0), axis=1)
    live_len = jnp.sum(jnp.where(hit, arrived[None, :, 1], 0), axis=1)
    key_rows, value_rows, extra_now = pl.pallas_call(
        unpack_kernel,
        out_shape=[
            jax.ShapeDtypeStruct(k_cache.shape, bf16),
            jax.ShapeDtypeStruct(v_cache.shape, bf16),
            jax.ShapeDtypeStruct((slot_count, extra_rows, kv_width), bf16),
        ],
        in_specs=[in_smem, in_vmem],
        out_specs=[in_vmem] * 3,
        cost_estimate=pl.CostEstimate(flops=0, bytes_accessed=4000000, transcendentals=0),
        compiler_params=pltpu.CompilerParams(vmem_limit_bytes=32 * 1024 * 1024),
    )(take, got_small)

    taps = conv_wx.shape[0]
    series_x = jnp.concatenate(
        [
            extra_now[:, :x_rows].reshape(slot_count, taps - 1, channels).transpose(1, 0, 2),
            x_in,
        ],
        axis=0,
    )
    series_bc = jnp.concatenate(
        [
            extra_now[:, x_rows:used].reshape(slot_count, taps - 1, -1).transpose(1, 0, 2),
            bc_in,
        ],
        axis=0,
    )
    window_x = series_x[STEPS:].transpose(1, 0, 2)
    window_bc = series_bc[STEPS:].transpose(1, 0, 2)

    def convolve(series, weights):
        total = sum(
            series[k : k + STEPS].astype(f32) * weights[k][None, None] for k in range(taps)
        )
        return jax.nn.silu(total)

    xs = convolve(series_x, conv_wx)
    conv_out_bc = convolve(series_bc, conv_wbc)
    b_vec, c_vec = conv_out_bc[..., :state_size], conv_out_bc[..., state_size:]
    delta = jax.nn.softplus(dt_in + dt_bias[None, None])
    decay = jnp.exp(-delta * a_rate[None, None])

    def spread(value):
        return jnp.repeat(value, head_size, axis=-1)

    reach = {}
    for first in range(STEPS):
        for last in range(first, STEPS):
            reach[first, last] = (
                decay[first] if first == last else reach[first, last - 1] * decay[last]
            )
    dots = {
        (i, t): jnp.sum(b_vec[i] * c_vec[t], axis=-1, keepdims=True)
        for t in range(STEPS)
        for i in range(t + 1)
    }
    y_new = []
    for t in range(STEPS):
        total = d_skip[None] + delta[t] * dots[t, t]
        part = xs[t] * spread(total)
        for i in range(t):
            part = part + xs[i] * spread(delta[i] * reach[i + 1, t] * dots[i, t])
        y_new.append(part)
    y_new = jnp.stack(y_new)
    grown = []
    for i in range(STEPS):
        scale = delta[i] if i == STEPS - 1 else delta[i] * reach[i + 1, STEPS - 1]
        grown.append(xs[i] * spread(scale))
    u_high, u_low = split_two(jnp.stack(grown, axis=1))
    b_high, b_low = split_two(b_vec.transpose(1, 0, 2))
    c_high, c_low = split_two(c_vec.transpose(1, 0, 2))
    u_all = jnp.pad(
        jnp.concatenate([u_high, u_high, u_low], axis=1), ((0, 0), (0, 16 - 3 * STEPS), (0, 0))
    )
    b_all = jnp.pad(
        jnp.concatenate([b_high, b_low, b_high], axis=1), ((0, 0), (0, 16 - 3 * STEPS), (0, 0))
    )
    eight = ((0, 0), (0, 8 - STEPS), (0, 0))
    c_all = jnp.concatenate([jnp.pad(c_high, eight), jnp.pad(c_low, eight)], axis=1)
    carry = reach[0, STEPS - 1].reshape(-1)
    gate = jax.nn.silu(z_in.astype(f32))
    y_scale = spread(jnp.stack([reach[0, t] for t in range(STEPS)]))
    gain = norm_gain.astype(f32)[None, None]

    kv_count = kv_width // HEAD_DIM
    query_group = QHEADS // KVHEADS
    positions = jnp.arange(cache_len, dtype=jnp.int32)
    for t in range(STEPS):
        written = positions[None, :, None] == (live_len + t)[:, None, None]
        key_rows = jnp.where(written, k_in[t][:, None, :], key_rows)
        value_rows = jnp.where(written, v_in[t][:, None, :], value_rows)
    queries = q_in.reshape(STEPS, slot_count, kv_count, query_group, HEAD_DIM)
    queries = queries.transpose(1, 2, 0, 3, 4).reshape(slot_count, kv_count, -1, HEAD_DIM)
    key_heads = key_rows.reshape(slot_count, cache_len, kv_count, HEAD_DIM)
    value_heads = value_rows.reshape(slot_count, cache_len, kv_count, HEAD_DIM)
    scores = jnp.einsum("skgd,sckd->skgc", queries, key_heads, preferred_element_type=f32)
    scores = scores * (1.0 / HEAD_DIM**0.5)
    row_step = jnp.arange(STEPS * query_group, dtype=jnp.int32) // query_group
    limit = live_len[:, None] + row_step[None, :]
    visible = positions[None, None, None, :] <= limit[:, None, :, None]
    scores = jnp.where(visible, scores, -jnp.inf)
    raised = jnp.exp(scores - jnp.max(scores, axis=3, keepdims=True))
    weights = (raised / jnp.sum(raised, axis=3, keepdims=True)).astype(bf16)
    mixed = jnp.einsum("skgc,sckd->skgd", weights, value_heads, preferred_element_type=f32)
    mixed = mixed.astype(bf16).reshape(slot_count, kv_count, STEPS, query_group, HEAD_DIM)
    mixed = mixed.transpose(2, 0, 1, 3, 4).reshape(STEPS * slot_count, -1)
    partial_value = jnp.dot(mixed, o_proj, preferred_element_type=f32)
    attn_all = lax.psum_scatter(
        partial_value.astype(bf16), "tp", scatter_dimension=1, tiled=True
    ).reshape(STEPS, slot_count, -1)

    final = None
    y_parts = []
    first = 0
    for heads, got in zip(CHUNKS, got_state):
        block = (1, heads, head_size, state_size)
        at = first // heads
        in_specs = [
            pl.BlockSpec(block, lambda s, take, carry: (take[s], 0, 0, 0)),
            pl.BlockSpec((1, 16, heads * head_size), lambda s, take, carry, at=at: (s, 0, at)),
            pl.BlockSpec((1, 16, state_size), lambda s, take, carry: (s, 0, 0)),
            pl.BlockSpec((1, 16, state_size), lambda s, take, carry: (s, 0, 0)),
        ]
        args = [take, carry, got, u_all, b_all, c_all]
        aliases = {}
        if final is not None:
            in_specs.append(anywhere)
            aliases = {len(args): 0}
            args.append(final)
        final, y_part = pl.pallas_call(
            functools.partial(state_kernel, first, head_count),
            grid_spec=pltpu.PrefetchScalarGridSpec(
                num_scalar_prefetch=2,
                grid=(slot_count,),
                in_specs=in_specs,
                out_specs=[
                    pl.BlockSpec(block, lambda s, take, carry, at=at: (s, at, 0, 0)),
                    pl.BlockSpec((1, 8, heads * head_size), lambda s, take, carry: (s, 0, 0)),
                ],
            ),
            out_shape=[
                jax.ShapeDtypeStruct(ssm_state.shape, bf16),
                jax.ShapeDtypeStruct((slot_count, 8, heads * head_size), f32),
            ],
            input_output_aliases=aliases,
            cost_estimate=pl.CostEstimate(
                flops=2 * 32 * got.size, bytes_accessed=4 * got.size, transcendentals=0
            ),
            compiler_params=pltpu.CompilerParams(vmem_limit_bytes=32 * 1024 * 1024),
        )(*args)
        y_parts.append(y_part[:, :STEPS].transpose(1, 0, 2))
        first += heads

    y_all = jnp.concatenate(y_parts, axis=2) * y_scale + y_new
    gated = y_all * gate
    normed = gated * lax.rsqrt(jnp.mean(gated * gated, axis=2, keepdims=True) + 1e-05)
    mamba = (normed * gain).astype(bf16)
    return (final, window_x, window_bc, key_rows, value_rows, mamba, attn_all)


def solution(mesh):
    in_specs = (
        P("inst", "tp", None, None),
        P("inst", None, "tp"),
        P("inst", None, "tp"),
        P("inst", None, "tp"),
        P("inst", None, "tp"),
        P("inst"),
        P("inst"),
        P("inst"),
        P(None, "inst", "tp"),
        P(None, "inst", "tp"),
        P(None, "inst", "tp"),
        P(None, "inst", "tp"),
        P(None, "inst", "tp"),
        P(None, "inst", "tp"),
        P(None, "inst", "tp"),
        P(None, "tp"),
        P(None, "tp"),
        P("tp"),
        P("tp"),
        P("tp"),
        P("tp"),
        P("tp", None),
    )
    out_specs = (
        P("inst", "tp", None, None),
        P("inst", None, "tp"),
        P("inst", None, "tp"),
        P("inst", None, "tp"),
        P("inst", None, "tp"),
        P(None, "inst", "tp"),
        P(None, "inst", "tp"),
    )
    return jax.shard_map(
        on_device, mesh=mesh, in_specs=in_specs, out_specs=out_specs, check_vma=False
    )
```

time: 366 us -> 491 us (1.34)
  Pallas kernels: 0 us -> 278 us
  other arithmetic: 65.6 us -> 9.99 us
  local copies, waits for them, and re-layouts: 57.4 us -> 15.5 us
  matrix products: 40.2 us -> 6.9 us
  waiting for transfers between devices: 159 us -> 148 us
  starting transfers between devices: 27.9 us -> 17.3 us
    pallas_call x0 -> x5, Pallas kernels: none -> 278 us  [the longest x1 256 us: on_device(): pl.pallas_call(functools.partial(pack_state_kernel, buckets), out_shape=[...]
    unnamed x122 -> x65, local copies, waits for them, and re-layouts: 50.4 us -> 5.12 us
    reduce_scatter x3 -> x1, waiting for transfers between devices: 52.5 us -> 10.6 us  [on_device(): lax.psum_scatter(partial_value.astype(bf16), 'tp', scatter_dimension=1, t...]
    reduce_sum x6 -> x3, other arithmetic: 34.8 us -> 1.21 us  [the longest x1 0.86 us: on_device(): jnp.mean(gated * gated, axis=2, keepdims=True) + 1e-05]
    all_to_all x6 -> x3, waiting for transfers between devices: 107 us -> 137 us  [the longest x2 137 us: on_device(): lax.all_to_all(part, 'inst', split_axis=0, concat_axis=0, tiled=True)]
    dot_general x13 -> x1, matrix products: 36 us -> 5.71 us  [on_device(): partial_value = jnp.dot(mixed, o_proj, preferred_element_type=f32)]
    convert_element_type x3 -> x5, other arithmetic: 18.3 us -> 0.62 us  [the longest x2 0.42 us: split_two(): return (high.astype(jnp.bfloat16), (value - high).astype(jnp.bfloat16))]
    all_to_all x6 -> x3, starting transfers between devices: 27.4 us -> 17.1 us  [the longest x2 9.78 us: on_device(): lax.all_to_all(part, 'inst', split_axis=0, concat_axis=0, tiled=True)]
  transfers between devices with their start and end apart: 9 -> 4, of which waited for: 8 -> 3; matrix products, arithmetic and copies ran while one was open for 22% -> 5% of each run, Pallas kernels for 0% -> 55%
where the time goes in v1:
time: 491 us; the launch traced here: 490 us
  Pallas kernels  278 us (57%)
  waiting for transfers between devices  148 us (30%)
  starting transfers between devices  17.3 us (4%)
  local copies, waits for them, and re-layouts  15.5 us (3%)
  between operations  14.8 us (3%)
  other arithmetic  9.99 us (2%)
  matrix products  6.9 us (1%)
    pallas_call x1, Pallas kernels, on_device(): pl.pallas_call(functools.partial(pack_state_kernel, buckets), out_shape=[...  256 us
    all_to_all x2, waiting for transfers between devices, on_device(): lax.all_to_all(part, 'inst', split_axis=0, concat_axis=0, tiled=True)  137 us
    pallas_call x2, Pallas kernels, on_device(): pl.pallas_call(functools.partial(state_kernel, first, head_count), grid_s...  19.6 us
    reduce_scatter x1, waiting for transfers between devices, on_device(): lax.psum_scatter(partial_value.astype(bf16), 'tp', scatter_dimension=1, t...  10.6 us
  transfers between devices with their start and end apart: 4, of which 3 were waited for; matrix products, arithmetic and copies ran while one was open for 5% of the time, Pallas kernels for 55%

profile of v1, /device:TPU:0, one launch (start us, length us, event | category | flops | bytes accessed | tf_op | source)
XLA Modules:
  0.0 490.4 jit_solution(15109370610825526085)
XLA Ops:
  7.2 0.8 convert_bitcast_fusion
  8.1 1.1 copy.81
  9.4 0.8 copy.82
  10.1 0.9 convert_reduce_fusion
  11.0 0.7 multiply_add_fusion.5
  11.9 1.7 shard_map.261
  13.7 7.3 %all-to-all-start = ((bf16[16,160,256]{2,1,0:T(8,128)(2,1)}), bf16[16,160,256]{2,1,0:T(8,128)(2,1)S(1)}, u32[]{:S(2)}, u32[]{:S(2)}) async-start(bf16[16,160,256]{2,1,0:T(8,128)(2,1)} %shard_map.261), calls=%async_computation | async-start | bytes 2621440 | tf_op jit(solution)/shard_map/all_to_all | solution.py:156
  20.9 256.2 %shard_map.262 = (bf16[16,24,64,128]{3,2,1,0:T(8,128)(2,1)}, bf16[16,8,64,128]{3,2,1,0:T(8,128)(2,1)}) custom-call(s32[16]{0:T(128)} %copy-done.4, bf16[14,32,64,128]{3,2,1,0:T(8,128)(2,1)} %state_ref.1), custom_call_target="tpu_custom_call" | custom-call | bytes 14680064 | tf_op jit(solution)/shard_map/pallas_call | solution.py:143
  277.2 6.1 %all-to-all-start.2 = ((bf16[16,24,64,128]{3,2,1,0:T(8,128)(2,1)}), bf16[16,24,64,128]{3,2,1,0:T(8,128)(2,1)}, u32[]{:S(2)}, u32[]{:S(2)}) async-start(bf16[16,24,64,128]{3,2,1,0:T(8,128)(2,1)} %get-tuple-element.18), calls=%async_computation.2 | async-start | bytes 12582912 | tf_op jit(solution)/shard_map/all_to_all | solution.py:158
  284.5 1.1 reshape.310
  288.2 0.8 convolution_convert_fusion.1
  289.2 131.8 %all-to-all-done.2.got_ref = bf16[16,24,64,128]{3,2,1,0:T(8,128)(2,1)} async-done(((bf16[16,24,64,128]{3,2,1,0:T(8,128)(2,1)}), bf16[16,24,64,128]{3,2,1,0:T(8,128)(2,1)}, u32[]{:S(2)}, u32[]{:S(2)}) %all-to-all-start.2) | async-done | bytes 6291488 | tf_op jit(solution)/shard_map/all_to_all | solution.py:158
  421.0 3.6 all-to-all-start.1
  424.9 5.7 %convolution_convert_fusion = bf16[42,4096]{1,0:T(8,128)(2,1)} fusion(bf16[42,1024]{1,0:T(8,128)(2,1)S(1)} %reshape.322, bf16[1024,4096]{1,0:T(8,128)(2,1)} %param.43), kind=kOutput, calls=%fused_computation.1 | convolution fusion | flops 352493568 | bytes 8818688 | tf_op jit(solution)/shard_map/dot_general | solution.py:272
  431.5 0.8 reshape.312
  432.5 0.8 reshape.313
  433.4 0.8 reshape.314
  434.4 0.8 reshape.315
  435.3 0.8 reshape.316
  436.6 0.8 reshape.308
  437.6 0.8 divide_multiply_fusion
  438.4 1.3 bitcast_multiply_fusion.2
  440.7 1.4 slice_multiply_fusion.4
  442.1 10.6 %reduce-scatter.2.cloned.1.call-done = bf16[42,1024]{1,0:T(8,128)(2,1)} async-done(((bf16[42,4096]{1,0:T(8,128)(2,1)}), bf16[42,1024]{1,0:T(8,128)(2,1)}) %reduce-scatter.2.cloned.1.call-update) | async-done | bytes 86032 | tf_op jit(solution)/shard_map/reduce_scatter | solution.py:273
  452.8 1.6 reshape.323
  454.4 12.5 %shard_map.264 = (bf16[14,32,64,128]{3,2,1,0:T(8,128)(2,1)}, f32[14,8,1536]{2,1,0:T(8,128)S(1)}) custom-call(s32[14]{0:T(128)S(1)} %get-tuple-element.60.take_ref, f32[448]{0:T(512)S(1)} %mul.296.carry_ref, bf16[16,24,64,128]{3,2,1,0:T(8,128)(2,1)} %all-to-all-done.2.got_ref, bf16[14,16,2048]{2,1,0:T(8,128)(2,1)S(1)} %fusion.9.u_ref, ...), custom_call_target="tpu_custom_call" | custom-call | flops 201326592 | bytes 12582912 | tf_op jit(solution)/shard_map/pallas_call | solution.py:295
  466.8 0.9 copy-done.2
  467.7 5.4 %all-to-all-done.1.got_ref = bf16[16,8,64,128]{3,2,1,0:T(8,128)(2,1)S(1)} async-done(((bf16[16,8,64,128]{3,2,1,0:T(8,128)(2,1)}), bf16[16,8,64,128]{3,2,1,0:T(8,128)(2,1)S(1)}, u32[]{:S(2)}, u32[]{:S(2)}) %all-to-all-start.1) | async-done | bytes 2097184 | tf_op jit(solution)/shard_map/all_to_all | solution.py:158
  473.1 7.1 %shard_map.265 = (bf16[14,32,64,128]{3,2,1,0:T(8,128)(2,1)}, f32[14,8,512]{2,1,0:T(8,128)S(1)}) custom-call(s32[14]{0:T(128)S(1)} %get-tuple-element.60.take_ref, f32[448]{0:T(512)S(1)} %mul.296.carry_ref, bf16[16,8,64,128]{3,2,1,0:T(8,128)(2,1)S(1)} %all-to-all-done.1.got_ref, ...), custom_call_target="tpu_custom_call", output_to_operand_aliasing={{0}: (6, {})} | custom-call | flops 67108864 | bytes 4194304 | tf_op jit(solution)/shard_map/pallas_call | solution.py:295
  480.4 0.9 multiply_reduce_fusion
  481.4 0.8 copy.98
  482.3 0.7 copy.118
  (129 shorter events, 8.2 us)
Async XLA Ops:
  7.2 4.8 copy-start
  7.2 4.8 copy-start.1
  11.8 1.8 copy-start.4
  13.7 263.5 %all-to-all-start = ((bf16[16,160,256]{2,1,0:T(8,128)(2,1)}), bf16[16,160,256]{2,1,0:T(8,128)(2,1)S(1)}, u32[]{:S(2)}, u32[]{:S(2)}) async-start(bf16[16,160,256]{2,1,0:T(8,128)(2,1)} %shard_map.261), calls=%async_computation | async-start | bytes 2621440 | tf_op jit(solution)/shard_map/all_to_all | solution.py:156
  277.1 6.2 %copy-start.18 = (bf16[3,14,1024]{2,1,0:T(8,128)(2,1)S(1)}, bf16[3,14,1024]{2,1,0:T(8,128)(2,1)}, u32[]{:S(2)}) copy-start(bf16[3,14,1024]{2,1,0:T(8,128)(2,1)} %param.34) | copy-start | bytes 258052
  277.1 6.4 %copy-start.19 = (bf16[3,14,256]{2,1,0:T(8,128)(2,1)S(1)}, bf16[3,14,256]{2,1,0:T(8,128)(2,1)}, u32[]{:S(2)}) copy-start(bf16[3,14,256]{2,1,0:T(8,128)(2,1)} %param.31) | copy-start | bytes 64516
  277.2 6.4 %copy-start.6 = (bf16[3,14,2048]{2,1,0:T(8,128)(2,1)S(1)}, bf16[3,14,2048]{2,1,0:T(8,128)(2,1)}, u32[]{:S(2)}) copy-start(bf16[3,14,2048]{2,1,0:T(8,128)(2,1)} %param.30) | copy-start | bytes 516100
  277.2 6.6 %copy-start.21 = (f32[3,14,32]{2,1,0:T(8,128)S(1)}, f32[3,14,32]{2,1,0:T(8,128)}, u32[]{:S(2)}) copy-start(f32[3,14,32]{2,1,0:T(8,128)} %param.33) | copy-start | bytes 16132
  277.2 6.6 %copy-start.27 = (f32[32]{0:T(128)S(1)}, f32[32]{0:T(128)}, u32[]{:S(2)}) copy-start(f32[32]{0:T(128)} %param.39) | copy-start | bytes 388
  277.2 6.6 %copy-start.28 = (f32[32]{0:T(128)S(1)}, f32[32]{0:T(128)}, u32[]{:S(2)}) copy-start(f32[32]{0:T(128)} %param.40) | copy-start | bytes 388
  277.2 143.8 %all-to-all-start.2 = ((bf16[16,24,64,128]{3,2,1,0:T(8,128)(2,1)}), bf16[16,24,64,128]{3,2,1,0:T(8,128)(2,1)}, u32[]{:S(2)}, u32[]{:S(2)}) async-start(bf16[16,24,64,128]{3,2,1,0:T(8,128)(2,1)} %get-tuple-element.18), calls=%async_computation.2 | async-start | bytes 12582912 | tf_op jit(solution)/shard_map/all_to_all | solution.py:158
  283.4 2.3 copy-start.24
  283.4 2.3 copy-start.25
  283.4 2.3 copy-start.22
  283.4 2.3 copy-start.23
  283.4 2.3 copy-start.20
  287.6 133.5 %copy-start.7 = (bf16[14,64,256]{2,1,0:T(8,128)(2,1)}, bf16[14,64,256]{2,1,0:T(8,128)(2,1)S(1)}, u32[]{:S(2)}) copy-start(bf16[14,64,256]{2,1,0:T(8,128)(2,1)S(1)} %get-tuple-element.132) | copy-start | bytes 1376260
  287.6 133.4 %copy-start.8 = (bf16[14,64,256]{2,1,0:T(8,128)(2,1)}, bf16[14,64,256]{2,1,0:T(8,128)(2,1)S(1)}, u32[]{:S(2)}) copy-start(bf16[14,64,256]{2,1,0:T(8,128)(2,1)S(1)} %get-tuple-element.131) | copy-start | bytes 1376260
  421.0 52.1 %all-to-all-start.1 = ((bf16[16,8,64,128]{3,2,1,0:T(8,128)(2,1)}), bf16[16,8,64,128]{3,2,1,0:T(8,128)(2,1)S(1)}, u32[]{:S(2)}, u32[]{:S(2)}) async-start(bf16[16,8,64,128]{3,2,1,0:T(8,128)(2,1)} %get-tuple-element.16), calls=%async_computation.1 | async-start | bytes 4194304 | tf_op jit(solution)/shard_map/all_to_all | solution.py:158
  424.7 6.4 %copy-start.26 = (f32[32]{0:T(128)S(1)}, f32[32]{0:T(128)}, u32[]{:S(2)}) copy-start(f32[32]{0:T(128)} %param.41) | copy-start | bytes 388
  424.7 28.1 %reduce-scatter.2.cloned.1.call-start = ((), (), s32[]{:S(2)}) async-start(), calls=%async_computation.4 | async-start | bytes 491520 | tf_op jit(solution)/shard_map/reduce_scatter | solution.py:273
  437.6 3.1 copy-start.9
  437.6 3.1 copy-start.10
  437.6 3.1 copy-start.11
  437.6 3.1 copy-start.12
  437.6 3.1 copy-start.13
  473.1 7.2 %copy-start.3 = (f32[14,8,1536]{2,1,0:T(8,128)S(1)}, f32[14,8,1536]{2,1,0:T(8,128)}, u32[]{:S(2)}) copy-start(f32[14,8,1536]{2,1,0:T(8,128)} %copy-done.2) | copy-start | bytes 2064388
  473.1 7.3 %copy-start.5 = (f32[3,14,2048]{2,0,1:T(4,128)S(1)}, f32[3,14,2048]{2,0,1:T(4,128)}, u32[]{:S(2)}) copy-start(f32[3,14,2048]{2,0,1:T(4,128)} %reshape.310) | copy-start | bytes 1032196
  473.1 7.3 %copy-start.14 = (f32[1,14,2048]{2,0,1:T(1,128)S(1)}, f32[1,14,2048]{2,0,1:T(1,128)}, u32[]{:S(2)}) copy-start(f32[1,14,2048]{2,0,1:T(1,128)} %get-tuple-element.71) | copy-start | bytes 344068
  473.1 7.3 %copy-start.15 = (f32[1,14,2048]{2,0,1:T(1,128)S(1)}, f32[1,14,2048]{2,0,1:T(1,128)}, u32[]{:S(2)}) copy-start(f32[1,14,2048]{2,0,1:T(1,128)} %get-tuple-element.72) | copy-start | bytes 344068
  473.1 7.3 %copy-start.16 = (f32[1,14,2048]{2,0,1:T(1,128)S(1)}, f32[1,14,2048]{2,0,1:T(1,128)}, u32[]{:S(2)}) copy-start(f32[1,14,2048]{2,0,1:T(1,128)} %get-tuple-element.73) | copy-start | bytes 344068
  473.1 7.3 %copy-start.17 = (bf16[3,14,2048]{2,1,0:T(8,128)(2,1)S(1)}, bf16[3,14,2048]{2,1,0:T(8,128)(2,1)}, u32[]{:S(2)}) copy-start(bf16[3,14,2048]{2,1,0:T(8,128)(2,1)} %param.32) | copy-start | bytes 516100
  (1 other events, 0.9 us)
Sparse Core Ops, SparseCore 0:
  430.7 22.0 reduce-scatter.1

commit v2 on v1

--- a/solution.py
+++ b/solution.py
@@ -22,22 +22,11 @@
         out_ref[b, 2 * cache_len :] = extra_ref[row_ref[b]]
 
 
-def pack_state_kernel(buckets, src_ref, state_ref, *rest):
-    outs, sems = rest[: len(CHUNKS)], rest[len(CHUNKS)]
-    copies = []
+def pack_state_kernel(src_ref, state_ref, *outs):
     at = 0
-    for c, heads in enumerate(CHUNKS):
-        for b in range(buckets):
-            copies.append(
-                pltpu.make_async_copy(
-                    state_ref.at[src_ref[b], pl.ds(at, heads)], outs[c].at[b], sems.at[c, b]
-                )
-            )
+    for heads, out in zip(CHUNKS, outs):
+        out[0] = state_ref[0, at : at + heads]
         at += heads
-    for copy in copies:
-        copy.start()
-    for copy in copies:
-        copy.wait()
 
 
 def unpack_kernel(take_ref, got_ref, k_ref, v_ref, extra_ref):
@@ -141,16 +130,27 @@
         compiler_params=pltpu.CompilerParams(vmem_limit_bytes=32 * 1024 * 1024),
     )(src, row, k_cache, v_cache, extra)
     packed = pl.pallas_call(
-        functools.partial(pack_state_kernel, buckets),
+        pack_state_kernel,
+        grid_spec=pltpu.PrefetchScalarGridSpec(
+            num_scalar_prefetch=1,
+            grid=(buckets,),
+            in_specs=[
+                pl.BlockSpec(
+                    (1, head_count, head_size, state_size), lambda b, src: (src[b], 0, 0, 0)
+                )
+            ],
+            out_specs=[
+                pl.BlockSpec((1, heads, head_size, state_size), lambda b, src: (b, 0, 0, 0))
+                for heads in CHUNKS
+            ],
+        ),
         out_shape=[
             jax.ShapeDtypeStruct((buckets, heads, head_size, state_size), bf16) for heads in CHUNKS
         ],
-        in_specs=[in_smem, anywhere],
-        out_specs=[anywhere] * len(CHUNKS),
-        scratch_shapes=[pltpu.SemaphoreType.DMA((len(CHUNKS), buckets))],
         cost_estimate=pl.CostEstimate(
             flops=0, bytes_accessed=4 * ssm_state.size, transcendentals=0
         ),
+        compiler_params=pltpu.CompilerParams(vmem_limit_bytes=32 * 1024 * 1024),
     )(src, ssm_state)
 
     got_small = lax.all_to_all(small, "inst", split_axis=0, concat_axis=0, tiled=True)

time: 491 us -> 265 us (0.54)
  Pallas kernels: 278 us -> 23.2 us
  waiting for transfers between devices: 148 us -> 170 us
  local copies, waits for them, and re-layouts: 15.5 us -> 22.5 us
    pallas_call x1, Pallas kernels: 256 us -> 1.32 us  [on_device(): pl.pallas_call(pack_state_kernel, grid_spec=pltpu.PrefetchScalarGridSpec(...]
    all_to_all x1, waiting for transfers between devices: 0.01 us -> 22.9 us  [on_device(): lax.all_to_all(small, 'inst', split_axis=0, concat_axis=0, tiled=True)]
    unnamed x65 -> x69, local copies, waits for them, and re-layouts: 5.12 us -> 12.2 us
  transfers between devices with their start and end apart: 4 -> 4, of which waited for: 3 -> 4; matrix products, arithmetic and copies ran while one was open for 5% -> 9% of each run, Pallas kernels for 55% -> 5%
where the time goes in v2:
time: 265 us; the launch traced here: 264 us
  waiting for transfers between devices  170 us (64%)
  Pallas kernels  23.2 us (9%)
  local copies, waits for them, and re-layouts  22.5 us (8%)
  starting transfers between devices  16 us (6%)
  between operations  14.8 us (6%)
  other arithmetic  9.98 us (4%)
  matrix products  6.9 us (3%)
    all_to_all x2, waiting for transfers between devices, on_device(): lax.all_to_all(part, 'inst', split_axis=0, concat_axis=0, tiled=True)  137 us
    all_to_all x1, waiting for transfers between devices, on_device(): lax.all_to_all(small, 'inst', split_axis=0, concat_axis=0, tiled=True)  22.9 us
    pallas_call x2, Pallas kernels, on_device(): pl.pallas_call(functools.partial(state_kernel, first, head_count), grid_s...  19.6 us
    unnamed x69, local copies, waits for them, and re-layouts  12.2 us
    reduce_scatter x1, waiting for transfers between devices, on_device(): lax.psum_scatter(partial_value.astype(bf16), 'tp', scatter_dimension=1, t...  10.7 us
    all_to_all x2, starting transfers between devices, on_device(): lax.all_to_all(part, 'inst', split_axis=0, concat_axis=0, tiled=True)  8.54 us
    all_to_all x1, starting transfers between devices, on_device(): lax.all_to_all(small, 'inst', split_axis=0, concat_axis=0, tiled=True)  7.28 us
    reshape x10, local copies, waits for them, and re-layouts, spread(): return jnp.repeat(value, head_size, axis=-1)  6.56 us
  transfers between devices with their start and end apart: 4, of which 4 were waited for; matrix products, arithmetic and copies ran while one was open for 9% of the time, Pallas kernels for 5%

profile of v2, /device:TPU:0, one launch (start us, length us, event | category | flops | bytes accessed | tf_op | source)
XLA Modules:
  0.0 263.9 jit_solution(10359067315218871472)
XLA Ops:
  8.1 1.1 copy.81
  10.1 0.9 convert_reduce_fusion
  11.9 1.7 shard_map.261
  13.6 7.3 %all-to-all-start = ((bf16[16,160,256]{2,1,0:T(8,128)(2,1)}), bf16[16,160,256]{2,1,0:T(8,128)(2,1)S(1)}, u32[]{:S(2)}, u32[]{:S(2)}) async-start(bf16[16,160,256]{2,1,0:T(8,128)(2,1)} %shard_map.261), calls=%async_computation | async-start | bytes 2621440 | tf_op jit(solution)/shard_map/all_to_all | solution.py:156
  20.9 3.1 %copy-done = bf16[14,32,64,128]{3,2,1,0:T(8,128)(2,1)S(1)} copy-done((bf16[14,32,64,128]{3,2,1,0:T(8,128)(2,1)S(1)}, bf16[14,32,64,128]{3,2,1,0:T(8,128)(2,1)}, u32[]{:S(2)}) %copy-start) | copy-done | bytes 7340056
  24.0 1.3 shard_map.262
  25.3 2.7 %copy-done.1 = bf16[16,24,64,128]{3,2,1,0:T(8,128)(2,1)} copy-done((bf16[16,24,64,128]{3,2,1,0:T(8,128)(2,1)}, bf16[16,24,64,128]{3,2,1,0:T(8,128)(2,1)S(1)}, u32[]{:S(2)}) %copy-start.1) | copy-done | bytes 6291480
  28.0 1.4 copy-done.2
  29.4 22.9 %all-to-all-done.got_ref = bf16[16,160,256]{2,1,0:T(8,128)(2,1)S(1)} async-done(((bf16[16,160,256]{2,1,0:T(8,128)(2,1)}), bf16[16,160,256]{2,1,0:T(8,128)(2,1)S(1)}, u32[]{:S(2)}, u32[]{:S(2)}) %all-to-all-start) | async-done | bytes 1310752 | tf_op jit(solution)/shard_map/all_to_all | solution.py:156
  52.3 4.9 %all-to-all-start.2 = ((bf16[16,24,64,128]{3,2,1,0:T(8,128)(2,1)}), bf16[16,24,64,128]{3,2,1,0:T(8,128)(2,1)}, u32[]{:S(2)}, u32[]{:S(2)}) async-start(bf16[16,24,64,128]{3,2,1,0:T(8,128)(2,1)} %copy-done.1), calls=%async_computation.2 | async-start | bytes 12582912 | tf_op jit(solution)/shard_map/all_to_all | solution.py:158
  58.4 1.1 reshape.310
  62.1 0.8 convolution_convert_fusion.1
  63.1 131.4 %all-to-all-done.2.got_ref = bf16[16,24,64,128]{3,2,1,0:T(8,128)(2,1)} async-done(((bf16[16,24,64,128]{3,2,1,0:T(8,128)(2,1)}), bf16[16,24,64,128]{3,2,1,0:T(8,128)(2,1)}, u32[]{:S(2)}, u32[]{:S(2)}) %all-to-all-start.2) | async-done | bytes 6291488 | tf_op jit(solution)/shard_map/all_to_all | solution.py:158
  194.5 3.6 %all-to-all-start.1 = ((bf16[16,8,64,128]{3,2,1,0:T(8,128)(2,1)}), bf16[16,8,64,128]{3,2,1,0:T(8,128)(2,1)S(1)}, u32[]{:S(2)}, u32[]{:S(2)}) async-start(bf16[16,8,64,128]{3,2,1,0:T(8,128)(2,1)} %copy-done.2), calls=%async_computation.1 | async-start | bytes 4194304 | tf_op jit(solution)/shard_map/all_to_all | solution.py:158
  198.4 5.7 %convolution_convert_fusion = bf16[42,4096]{1,0:T(8,128)(2,1)} fusion(bf16[42,1024]{1,0:T(8,128)(2,1)S(1)} %reshape.322, bf16[1024,4096]{1,0:T(8,128)(2,1)} %param.43), kind=kOutput, calls=%fused_computation.1 | convolution fusion | flops 352493568 | bytes 8818688 | tf_op jit(solution)/shard_map/dot_general | solution.py:272
  205.1 0.8 reshape.312
  206.0 0.8 reshape.313
  206.9 0.8 reshape.314
  207.9 0.8 reshape.315
  208.8 0.8 reshape.316
  210.1 0.8 reshape.308
  211.1 0.8 divide_multiply_fusion
  211.9 1.3 bitcast_multiply_fusion.2
  214.2 1.4 slice_multiply_fusion.4
  215.6 10.7 %reduce-scatter.2.cloned.1.call-done = bf16[42,1024]{1,0:T(8,128)(2,1)} async-done(((bf16[42,4096]{1,0:T(8,128)(2,1)}), bf16[42,1024]{1,0:T(8,128)(2,1)}) %reduce-scatter.2.cloned.1.call-update) | async-done | bytes 86032 | tf_op jit(solution)/shard_map/reduce_scatter | solution.py:273
  226.3 1.6 reshape.323
  227.9 12.5 %shard_map.264 = (bf16[14,32,64,128]{3,2,1,0:T(8,128)(2,1)}, f32[14,8,1536]{2,1,0:T(8,128)S(1)}) custom-call(s32[14]{0:T(128)S(1)} %get-tuple-element.60.take_ref, f32[448]{0:T(512)S(1)} %mul.296.carry_ref, bf16[16,24,64,128]{3,2,1,0:T(8,128)(2,1)} %all-to-all-done.2.got_ref, bf16[14,16,2048]{2,1,0:T(8,128)(2,1)S(1)} %fusion.9.u_ref, ...), custom_call_target="tpu_custom_call" | custom-call | flops 201326592 | bytes 12582912 | tf_op jit(solution)/shard_map/pallas_call | solution.py:295
  240.3 0.8 copy-done.5
  241.2 5.4 %all-to-all-done.1.got_ref = bf16[16,8,64,128]{3,2,1,0:T(8,128)(2,1)S(1)} async-done(((bf16[16,8,64,128]{3,2,1,0:T(8,128)(2,1)}), bf16[16,8,64,128]{3,2,1,0:T(8,128)(2,1)S(1)}, u32[]{:S(2)}, u32[]{:S(2)}) %all-to-all-start.1) | async-done | bytes 2097184 | tf_op jit(solution)/shard_map/all_to_all | solution.py:158
  246.6 7.1 %shard_map.265 = (bf16[14,32,64,128]{3,2,1,0:T(8,128)(2,1)}, f32[14,8,512]{2,1,0:T(8,128)S(1)}) custom-call(s32[14]{0:T(128)S(1)} %get-tuple-element.60.take_ref, f32[448]{0:T(512)S(1)} %mul.296.carry_ref, bf16[16,8,64,128]{3,2,1,0:T(8,128)(2,1)S(1)} %all-to-all-done.1.got_ref, ...), custom_call_target="tpu_custom_call", output_to_operand_aliasing={{0}: (6, {})} | custom-call | flops 67108864 | bytes 4194304 | tf_op jit(solution)/shard_map/pallas_call | solution.py:295
  253.9 0.9 multiply_reduce_fusion
  254.9 0.8 copy.98
  (133 shorter events, 11.0 us)
Async XLA Ops:
  7.2 4.8 %copy-start.3 = (bf16[14,64,256]{2,1,0:T(8,128)(2,1)S(1)}, bf16[14,64,256]{2,1,0:T(8,128)(2,1)}, u32[]{:S(2)}) copy-start(bf16[14,64,256]{2,1,0:T(8,128)(2,1)} %k_ref.1) | copy-start | bytes 1376260
  7.2 4.8 %copy-start.4 = (bf16[14,64,256]{2,1,0:T(8,128)(2,1)S(1)}, bf16[14,64,256]{2,1,0:T(8,128)(2,1)}, u32[]{:S(2)}) copy-start(bf16[14,64,256]{2,1,0:T(8,128)(2,1)} %v_ref.1) | copy-start | bytes 1376260
  13.6 38.7 %all-to-all-start = ((bf16[16,160,256]{2,1,0:T(8,128)(2,1)}), bf16[16,160,256]{2,1,0:T(8,128)(2,1)S(1)}, u32[]{:S(2)}, u32[]{:S(2)}) async-start(bf16[16,160,256]{2,1,0:T(8,128)(2,1)} %shard_map.261), calls=%async_computation | async-start | bytes 2621440 | tf_op jit(solution)/shard_map/all_to_all | solution.py:156
  20.9 3.1 %copy-start = (bf16[14,32,64,128]{3,2,1,0:T(8,128)(2,1)S(1)}, bf16[14,32,64,128]{3,2,1,0:T(8,128)(2,1)}, u32[]{:S(2)}) copy-start(bf16[14,32,64,128]{3,2,1,0:T(8,128)(2,1)} %state_ref.1) | copy-start | bytes 22020100
  25.3 2.7 %copy-start.1 = (bf16[16,24,64,128]{3,2,1,0:T(8,128)(2,1)}, bf16[16,24,64,128]{3,2,1,0:T(8,128)(2,1)S(1)}, u32[]{:S(2)}) copy-start(bf16[16,24,64,128]{3,2,1,0:T(8,128)(2,1)S(1)} %get-tuple-element.18) | copy-start | bytes 18874372
  52.3 5.0 %copy-start.20 = (bf16[3,14,1024]{2,1,0:T(8,128)(2,1)S(1)}, bf16[3,14,1024]{2,1,0:T(8,128)(2,1)}, u32[]{:S(2)}) copy-start(bf16[3,14,1024]{2,1,0:T(8,128)(2,1)} %param.34) | copy-start | bytes 258052
  52.3 5.1 %copy-start.21 = (bf16[3,14,256]{2,1,0:T(8,128)(2,1)S(1)}, bf16[3,14,256]{2,1,0:T(8,128)(2,1)}, u32[]{:S(2)}) copy-start(bf16[3,14,256]{2,1,0:T(8,128)(2,1)} %param.31) | copy-start | bytes 64516
  52.3 5.2 %copy-start.8 = (bf16[3,14,2048]{2,1,0:T(8,128)(2,1)S(1)}, bf16[3,14,2048]{2,1,0:T(8,128)(2,1)}, u32[]{:S(2)}) copy-start(bf16[3,14,2048]{2,1,0:T(8,128)(2,1)} %param.30) | copy-start | bytes 516100
  52.3 5.3 %copy-start.23 = (f32[3,14,32]{2,1,0:T(8,128)S(1)}, f32[3,14,32]{2,1,0:T(8,128)}, u32[]{:S(2)}) copy-start(f32[3,14,32]{2,1,0:T(8,128)} %param.33) | copy-start | bytes 16132
  52.3 5.3 %copy-start.29 = (f32[32]{0:T(128)S(1)}, f32[32]{0:T(128)}, u32[]{:S(2)}) copy-start(f32[32]{0:T(128)} %param.39) | copy-start | bytes 388
  52.3 5.3 %copy-start.30 = (f32[32]{0:T(128)S(1)}, f32[32]{0:T(128)}, u32[]{:S(2)}) copy-start(f32[32]{0:T(128)} %param.40) | copy-start | bytes 388
  52.3 142.2 %all-to-all-start.2 = ((bf16[16,24,64,128]{3,2,1,0:T(8,128)(2,1)}), bf16[16,24,64,128]{3,2,1,0:T(8,128)(2,1)}, u32[]{:S(2)}, u32[]{:S(2)}) async-start(bf16[16,24,64,128]{3,2,1,0:T(8,128)(2,1)} %copy-done.1), calls=%async_computation.2 | async-start | bytes 12582912 | tf_op jit(solution)/shard_map/all_to_all | solution.py:158
  57.3 2.3 copy-start.26
  57.3 2.3 copy-start.24
  57.3 2.3 copy-start.25
  57.3 2.3 copy-start.22
  61.5 133.0 %copy-start.9 = (bf16[14,64,256]{2,1,0:T(8,128)(2,1)}, bf16[14,64,256]{2,1,0:T(8,128)(2,1)S(1)}, u32[]{:S(2)}) copy-start(bf16[14,64,256]{2,1,0:T(8,128)(2,1)S(1)} %get-tuple-element.132) | copy-start | bytes 1376260
  61.5 133.0 %copy-start.10 = (bf16[14,64,256]{2,1,0:T(8,128)(2,1)}, bf16[14,64,256]{2,1,0:T(8,128)(2,1)S(1)}, u32[]{:S(2)}) copy-start(bf16[14,64,256]{2,1,0:T(8,128)(2,1)S(1)} %get-tuple-element.131) | copy-start | bytes 1376260
  194.5 52.0 %all-to-all-start.1 = ((bf16[16,8,64,128]{3,2,1,0:T(8,128)(2,1)}), bf16[16,8,64,128]{3,2,1,0:T(8,128)(2,1)S(1)}, u32[]{:S(2)}, u32[]{:S(2)}) async-start(bf16[16,8,64,128]{3,2,1,0:T(8,128)(2,1)} %copy-done.2), calls=%async_computation.1 | async-start | bytes 4194304 | tf_op jit(solution)/shard_map/all_to_all | solution.py:158
  198.2 6.4 %copy-start.28 = (f32[32]{0:T(128)S(1)}, f32[32]{0:T(128)}, u32[]{:S(2)}) copy-start(f32[32]{0:T(128)} %param.41) | copy-start | bytes 388
  198.2 28.1 %reduce-scatter.2.cloned.1.call-start = ((), (), s32[]{:S(2)}) async-start(), calls=%async_computation.4 | async-start | bytes 491520 | tf_op jit(solution)/shard_map/reduce_scatter | solution.py:273
  211.0 3.1 %copy-start.11 = (f32[1,14,2048]{2,0,1:T(1,128)S(1)}, f32[1,14,2048]{2,0,1:T(1,128)}, u32[]{:S(2)}) copy-start(f32[1,14,2048]{2,0,1:T(1,128)} %reshape.312) | copy-start | bytes 344068
  211.1 3.1 %copy-start.12 = (f32[1,14,2048]{2,0,1:T(1,128)S(1)}, f32[1,14,2048]{2,0,1:T(1,128)}, u32[]{:S(2)}) copy-start(f32[1,14,2048]{2,0,1:T(1,128)} %reshape.313) | copy-start | bytes 344068
  211.1 3.1 %copy-start.13 = (f32[1,14,2048]{2,0,1:T(1,128)S(1)}, f32[1,14,2048]{2,0,1:T(1,128)}, u32[]{:S(2)}) copy-start(f32[1,14,2048]{2,0,1:T(1,128)} %reshape.314) | copy-start | bytes 344068
  211.1 3.1 %copy-start.14 = (f32[1,14,2048]{2,0,1:T(1,128)S(1)}, f32[1,14,2048]{2,0,1:T(1,128)}, u32[]{:S(2)}) copy-start(f32[1,14,2048]{2,0,1:T(1,128)} %reshape.315) | copy-start | bytes 344068
  211.1 3.1 %copy-start.15 = (f32[1,14,2048]{2,0,1:T(1,128)S(1)}, f32[1,14,2048]{2,0,1:T(1,128)}, u32[]{:S(2)}) copy-start(f32[1,14,2048]{2,0,1:T(1,128)} %reshape.316) | copy-start | bytes 344068
  246.6 7.2 %copy-start.6 = (f32[14,8,1536]{2,1,0:T(8,128)S(1)}, f32[14,8,1536]{2,1,0:T(8,128)}, u32[]{:S(2)}) copy-start(f32[14,8,1536]{2,1,0:T(8,128)} %copy-done.5) | copy-start | bytes 2064388
  246.6 7.3 %copy-start.7 = (f32[3,14,2048]{2,0,1:T(4,128)S(1)}, f32[3,14,2048]{2,0,1:T(4,128)}, u32[]{:S(2)}) copy-start(f32[3,14,2048]{2,0,1:T(4,128)} %reshape.310) | copy-start | bytes 1032196
  246.6 7.3 %copy-start.16 = (f32[1,14,2048]{2,0,1:T(1,128)S(1)}, f32[1,14,2048]{2,0,1:T(1,128)}, u32[]{:S(2)}) copy-start(f32[1,14,2048]{2,0,1:T(1,128)} %get-tuple-element.71) | copy-start | bytes 344068
  246.6 7.3 %copy-start.17 = (f32[1,14,2048]{2,0,1:T(1,128)S(1)}, f32[1,14,2048]{2,0,1:T(1,128)}, u32[]{:S(2)}) copy-start(f32[1,14,2048]{2,0,1:T(1,128)} %get-tuple-element.72) | copy-start | bytes 344068
  246.6 7.3 %copy-start.18 = (f32[1,14,2048]{2,0,1:T(1,128)S(1)}, f32[1,14,2048]{2,0,1:T(1,128)}, u32[]{:S(2)}) copy-start(f32[1,14,2048]{2,0,1:T(1,128)} %get-tuple-element.73) | copy-start | bytes 344068
  246.6 7.3 %copy-start.19 = (bf16[3,14,2048]{2,1,0:T(8,128)(2,1)S(1)}, bf16[3,14,2048]{2,1,0:T(8,128)(2,1)}, u32[]{:S(2)}) copy-start(bf16[3,14,2048]{2,1,0:T(8,128)(2,1)} %param.32) | copy-start | bytes 516100
  (3 other events, 4.5 us)
Sparse Core Ops, SparseCore 0:
  204.3 21.9 reduce-scatter.1

commit v3 on v2

--- a/solution.py
+++ b/solution.py
@@ -11,7 +11,7 @@
 QHEADS = 32
 KVHEADS = 8
 HEAD_DIM = 128
-CHUNKS = (24, 8)
+CHUNKS = (28, 4)
 
 
 def pack_small_kernel(src_ref, row_ref, k_ref, v_ref, extra_ref, out_ref):
@@ -39,19 +39,26 @@
 
 def state_kernel(first, head_count, take_ref, carry_ref, got_ref, u_ref, b_ref, c_ref, *rest):
     final_ref, y_ref = rest[-2:]
-    slot = pl.program_id(0)
+    slots = final_ref.shape[0]
     heads, size, width = got_ref.shape[1:]
-    old = got_ref[0].reshape(heads * size, width)
-    both = lax.dot_general(
-        c_ref[0], old, (((1,), (1,)), ((), ())), preferred_element_type=jnp.float32
-    )
-    y_ref[0] = both[:8] + both[8:]
-    added = lax.dot_general(
-        u_ref[0], b_ref[0], (((0,), (0,)), ((), ())), preferred_element_type=jnp.float32
-    )
-    for h in range(heads):
-        kept = got_ref[0, h].astype(jnp.float32) * carry_ref[slot * head_count + first + h]
-        final_ref[0, h] = (kept + added[h * size : (h + 1) * size]).astype(jnp.bfloat16)
+    for s in range(slots):
+        slot = pl.program_id(0) * slots + s
+        source = 0 if slots == 1 else take_ref[slot]
+        old = got_ref[source]
+        both = lax.dot_general(
+            c_ref[s],
+            old.reshape(heads * size, width),
+            (((1,), (1,)), ((), ())),
+            preferred_element_type=jnp.float32,
+        )
+        y_ref[s] = both[:8] + both[8:]
+        added = lax.dot_general(
+            u_ref[s], b_ref[s], (((0,), (0,)), ((), ())), preferred_element_type=jnp.float32
+        )
+        for h in range(heads):
+            kept = old[h].astype(jnp.float32) * carry_ref[slot * head_count + first + h]
+            new = kept + added[h * size : (h + 1) * size]
+            final_ref[s, h] = new.astype(jnp.bfloat16)
 
 
 def split_two(value):
@@ -154,9 +161,6 @@
     )(src, ssm_state)
 
     got_small = lax.all_to_all(small, "inst", split_axis=0, concat_axis=0, tiled=True)
-    got_state = [
-        lax.all_to_all(part, "inst", split_axis=0, concat_axis=0, tiled=True) for part in packed
-    ]
 
     arrived = got_small[:, 2 * cache_len + used, :2].astype(jnp.int32)
     hit = arrived[None, :, 0] == slot_ids[:, None]
@@ -274,17 +278,31 @@
         partial_value.astype(bf16), "tp", scatter_dimension=1, tiled=True
     ).reshape(STEPS, slot_count, -1)
 
+    tied = (packed[-1], attn_all, take, carry, u_all, b_all, c_all, y_new, y_scale, gate)
+    tied = lax.optimization_barrier((*tied, window_x, window_bc, gain))
+    last_part, attn_all, take, carry, u_all, b_all, c_all, y_new, y_scale, gate = tied[:10]
+    window_x, window_bc, gain = tied[10:]
+    got_state = [
+        lax.all_to_all(part, "inst", split_axis=0, concat_axis=0, tiled=True)
+        for part in [*packed[:-1], last_part]
+    ]
+
     final = None
     y_parts = []
     first = 0
     for heads, got in zip(CHUNKS, got_state):
-        block = (1, heads, head_size, state_size)
         at = first // heads
+        slots = slot_count if final is not None else 1
+        block = (slots, heads, head_size, state_size)
+        if slots == 1:
+            got_spec = pl.BlockSpec(block, lambda s, take, carry: (take[s], 0, 0, 0))
+        else:
+            got_spec = pl.BlockSpec(got.shape, lambda s, take, carry: (0, 0, 0, 0))
         in_specs = [
-            pl.BlockSpec(block, lambda s, take, carry: (take[s], 0, 0, 0)),
-            pl.BlockSpec((1, 16, heads * head_size), lambda s, take, carry, at=at: (s, 0, at)),
-            pl.BlockSpec((1, 16, state_size), lambda s, take, carry: (s, 0, 0)),
-            pl.BlockSpec((1, 16, state_size), lambda s, take, carry: (s, 0, 0)),
+            got_spec,
+            pl.BlockSpec((slots, 16, heads * head_size), lambda s, take, carry, at=at: (s, 0, at)),
+            pl.BlockSpec((slots, 16, state_size), lambda s, take, carry: (s, 0, 0)),
+            pl.BlockSpec((slots, 16, state_size), lambda s, take, carry: (s, 0, 0)),
         ]
         args = [take, carry, got, u_all, b_all, c_all]
         aliases = {}
@@ -296,11 +314,11 @@
             functools.partial(state_kernel, first, head_count),
             grid_spec=pltpu.PrefetchScalarGridSpec(
                 num_scalar_prefetch=2,
-                grid=(slot_count,),
+                grid=(slot_count // slots,),
                 in_specs=in_specs,
                 out_specs=[
                     pl.BlockSpec(block, lambda s, take, carry, at=at: (s, at, 0, 0)),
-                    pl.BlockSpec((1, 8, heads * head_size), lambda s, take, carry: (s, 0, 0)),
+                    pl.BlockSpec((slots, 8, heads * head_size), lambda s, take, carry: (s, 0, 0)),
                 ],
             ),
             out_shape=[

time: 265 us -> 259 us (0.977)
  waiting for transfers between devices: 170 us -> 161 us
  other arithmetic: 9.98 us -> 13.8 us
    all_to_all x2, waiting for transfers between devices: 137 us -> 123 us  [on_device(): lax.all_to_all(part, 'inst', split_axis=0, concat_axis=0, tiled=True)]
    reduce_scatter x1, waiting for transfers between devices: 10.7 us -> 18.2 us  [on_device(): lax.psum_scatter(partial_value.astype(bf16), 'tp', scatter_dimension=1, t...]
    pallas_call x2, Pallas kernels: 19.6 us -> 15 us  [on_device(): pl.pallas_call(functools.partial(state_kernel, first, head_count), grid_s...]
    pallas_call x1, Pallas kernels: 1.32 us -> 5.9 us  [on_device(): pl.pallas_call(pack_state_kernel, grid_spec=pltpu.PrefetchScalarGridSpec(...]
    all_to_all x1, waiting for transfers between devices: 22.9 us -> 19.4 us  [on_device(): lax.all_to_all(small, 'inst', split_axis=0, concat_axis=0, tiled=True)]
    unnamed x69 -> x85, local copies, waits for them, and re-layouts: 12.2 us -> 11.3 us
  transfers between devices with their start and end apart: 4 -> 4, of which waited for: 4 -> 4; matrix products, arithmetic and copies ran while one was open for 9% -> 12% of each run, Pallas kernels for 5% -> 8%
where the time goes in v3:
time: 259 us; the launch traced here: 258 us
  waiting for transfers between devices  161 us (62%)
  Pallas kernels  23.2 us (9%)
  local copies, waits for them, and re-layouts  21.9 us (8%)
  starting transfers between devices  15.9 us (6%)
  between operations  14.8 us (6%)
  other arithmetic  13.8 us (5%)
  matrix products  8 us (3%)
    all_to_all x2, waiting for transfers between devices, on_device(): lax.all_to_all(part, 'inst', split_axis=0, concat_axis=0, tiled=True)  123 us
    all_to_all x1, waiting for transfers between devices, on_device(): lax.all_to_all(small, 'inst', split_axis=0, concat_axis=0, tiled=True)  19.4 us
    reduce_scatter x1, waiting for transfers between devices, on_device(): lax.psum_scatter(partial_value.astype(bf16), 'tp', scatter_dimension=1, t...  18.2 us
    pallas_call x2, Pallas kernels, on_device(): pl.pallas_call(functools.partial(state_kernel, first, head_count), grid_s...  15 us
    unnamed x85, local copies, waits for them, and re-layouts  11.3 us
    all_to_all x2, starting transfers between devices, on_device(): lax.all_to_all(part, 'inst', split_axis=0, concat_axis=0, tiled=True)  8.63 us
    all_to_all x1, starting transfers between devices, on_device(): lax.all_to_all(small, 'inst', split_axis=0, concat_axis=0, tiled=True)  7.28 us
    pallas_call x1, Pallas kernels, on_device(): pl.pallas_call(pack_state_kernel, grid_spec=pltpu.PrefetchScalarGridSpec(...  5.9 us
  transfers between devices with their start and end apart: 4, of which 4 were waited for; matrix products, arithmetic and copies ran while one was open for 12% of the time, Pallas kernels for 8%

profile of v3, /device:TPU:0, one launch (start us, length us, event | category | flops | bytes accessed | tf_op | source)
XLA Modules:
  0.0 258.4 jit_solution(485987982757695502)
XLA Ops:
  7.2 0.8 convert_bitcast_fusion
  8.1 1.1 copy.81
  9.4 0.8 copy.82
  10.1 0.9 convert_reduce_fusion
  11.9 1.7 shard_map.262
  13.6 7.3 %all-to-all-start = ((bf16[16,160,256]{2,1,0:T(8,128)(2,1)}), bf16[16,160,256]{2,1,0:T(8,128)(2,1)S(1)}, u32[]{:S(2)}, u32[]{:S(2)}) async-start(bf16[16,160,256]{2,1,0:T(8,128)(2,1)} %shard_map.262), calls=%async_computation | async-start | bytes 2621440 | tf_op jit(solution)/shard_map/all_to_all | solution.py:163
  20.9 3.1 %copy-done.1 = bf16[14,32,64,128]{3,2,1,0:T(8,128)(2,1)S(1)} copy-done((bf16[14,32,64,128]{3,2,1,0:T(8,128)(2,1)S(1)}, bf16[14,32,64,128]{3,2,1,0:T(8,128)(2,1)}, u32[]{:S(2)}) %copy-start.1) | copy-done | bytes 7340056
  24.0 5.9 %shard_map.261 = (bf16[16,28,64,128]{3,2,1,0:T(8,128)(2,1)S(1)}, bf16[16,4,64,128]{3,2,1,0:T(8,128)(2,1)}) custom-call(s32[16]{0:T(128)S(1)} %compare_select_fusion.1.src_ref, bf16[14,32,64,128]{3,2,1,0:T(8,128)(2,1)S(1)} %copy-done.1), custom_call_target="tpu_custom_call" | custom-call | bytes 14680064 | tf_op jit(solution)/shard_map/pallas_call | solution.py:139
  29.9 3.0 %copy-done = bf16[16,28,64,128]{3,2,1,0:T(8,128)(2,1)} copy-done((bf16[16,28,64,128]{3,2,1,0:T(8,128)(2,1)}, bf16[16,28,64,128]{3,2,1,0:T(8,128)(2,1)S(1)}, u32[]{:S(2)}) %copy-start) | copy-done | bytes 7340056
  32.9 19.4 %all-to-all-done.got_ref = bf16[16,160,256]{2,1,0:T(8,128)(2,1)S(1)} async-done(((bf16[16,160,256]{2,1,0:T(8,128)(2,1)}), bf16[16,160,256]{2,1,0:T(8,128)(2,1)S(1)}, u32[]{:S(2)}, u32[]{:S(2)}) %all-to-all-start) | async-done | bytes 1310752 | tf_op jit(solution)/shard_map/all_to_all | solution.py:163
  52.3 5.0 %all-to-all-start.2 = ((bf16[16,28,64,128]{3,2,1,0:T(8,128)(2,1)}), bf16[16,28,64,128]{3,2,1,0:T(8,128)(2,1)}, u32[]{:S(2)}, u32[]{:S(2)}) async-start(bf16[16,28,64,128]{3,2,1,0:T(8,128)(2,1)} %copy-done), calls=%async_computation.3 | async-start | bytes 14680064 | tf_op jit(solution)/shard_map/all_to_all | solution.py:286
  58.7 0.7 copy.86
  63.0 1.1 convert_multiply_fusion
  65.6 1.0 divide_multiply_fusion.1
  66.8 0.7 multiply_add_fusion.4
  69.0 0.8 reshape.320
  69.9 0.8 reshape.321
  70.9 0.8 reshape.313
  71.9 0.8 reshape.314
  73.2 1.2 select_select_fusion.1
  75.0 1.9 convolution_convert_fusion.1
  77.1 5.8 %convolution_convert_fusion = bf16[42,4096]{1,0:T(8,128)(2,1)} fusion(bf16[42,1024]{1,0:T(8,128)(2,1)S(1)} %reshape.310, bf16[1024,4096]{1,0:T(8,128)(2,1)} %param.43), kind=kOutput, calls=%fused_computation.1 | convolution fusion | flops 352493568 | bytes 8818688 | tf_op jit(solution)/shard_map/dot_general | solution.py:276
  83.1 0.8 divide_multiply_fusion
  84.9 1.1 pad_maximum_fusion.1
  87.0 18.2 %reduce-scatter.2.cloned.1.call-done = bf16[42,1024]{1,0:T(8,128)(2,1)} async-done(((bf16[42,4096]{1,0:T(8,128)(2,1)}), bf16[42,1024]{1,0:T(8,128)(2,1)}) %reduce-scatter.2.cloned.1.call-update) | async-done | bytes 86032 | tf_op jit(solution)/shard_map/reduce_scatter | solution.py:277
  105.2 1.6 reshape.311
  106.8 110.3 %all-to-all-done.2.got_ref = bf16[16,28,64,128]{3,2,1,0:T(8,128)(2,1)} async-done(((bf16[16,28,64,128]{3,2,1,0:T(8,128)(2,1)}), bf16[16,28,64,128]{3,2,1,0:T(8,128)(2,1)}, u32[]{:S(2)}, u32[]{:S(2)}) %all-to-all-start.2) | async-done | bytes 7340064 | tf_op jit(solution)/shard_map/all_to_all | solution.py:286
  217.1 3.6 %all-to-all-start.1 = ((bf16[16,4,64,128]{3,2,1,0:T(8,128)(2,1)}), bf16[16,4,64,128]{3,2,1,0:T(8,128)(2,1)S(1)}, u32[]{:S(2)}, u32[]{:S(2)}) async-start(bf16[16,4,64,128]{3,2,1,0:T(8,128)(2,1)} %get-tuple-element.35), calls=%async_computation.2 | async-start | bytes 2097152 | tf_op jit(solution)/shard_map/all_to_all | solution.py:286
  220.7 13.0 %shard_map.264 = (bf16[14,32,64,128]{3,2,1,0:T(8,128)(2,1)}, f32[14,8,1792]{2,1,0:T(8,128)S(1)}) custom-call(s32[14]{0:T(128)S(1)} %get-tuple-element.33.take_ref, f32[448]{0:T(512)S(1)} %mul.301.carry_ref, bf16[16,28,64,128]{3,2,1,0:T(8,128)(2,1)} %all-to-all-done.2.got_ref, bf16[14,16,2048]{2,1,0:T(8,128)(2,1)S(1)} %fusion.9.u_ref, ...), custom_call_target="tpu_custom_call" | custom-call | flops 234881024 | bytes 14680064 | tf_op jit(solution)/shard_map/pallas_call | solution.py:313
  233.7 12.9 %all-to-all-done.1.got_ref = bf16[16,4,64,128]{3,2,1,0:T(8,128)(2,1)S(1)} async-done(((bf16[16,4,64,128]{3,2,1,0:T(8,128)(2,1)}), bf16[16,4,64,128]{3,2,1,0:T(8,128)(2,1)S(1)}, u32[]{:S(2)}, u32[]{:S(2)}) %all-to-all-start.1) | async-done | bytes 1048608 | tf_op jit(solution)/shard_map/all_to_all | solution.py:286
  246.6 2.0 shard_map.265
  249.4 0.8 copy.98
  (151 shorter events, 14.8 us)
Async XLA Ops:
  7.2 4.8 %copy-start.2 = (bf16[14,64,256]{2,1,0:T(8,128)(2,1)S(1)}, bf16[14,64,256]{2,1,0:T(8,128)(2,1)}, u32[]{:S(2)}) copy-start(bf16[14,64,256]{2,1,0:T(8,128)(2,1)} %k_ref.1) | copy-start | bytes 1376260
  7.2 4.8 %copy-start.3 = (bf16[14,64,256]{2,1,0:T(8,128)(2,1)S(1)}, bf16[14,64,256]{2,1,0:T(8,128)(2,1)}, u32[]{:S(2)}) copy-start(bf16[14,64,256]{2,1,0:T(8,128)(2,1)} %v_ref.1) | copy-start | bytes 1376260
  13.6 38.7 %all-to-all-start = ((bf16[16,160,256]{2,1,0:T(8,128)(2,1)}), bf16[16,160,256]{2,1,0:T(8,128)(2,1)S(1)}, u32[]{:S(2)}, u32[]{:S(2)}) async-start(bf16[16,160,256]{2,1,0:T(8,128)(2,1)} %shard_map.262), calls=%async_computation | async-start | bytes 2621440 | tf_op jit(solution)/shard_map/all_to_all | solution.py:163
  52.3 5.2 %copy-start.16 = (bf16[3,14,256]{2,1,0:T(8,128)(2,1)S(1)}, bf16[3,14,256]{2,1,0:T(8,128)(2,1)}, u32[]{:S(2)}) copy-start(bf16[3,14,256]{2,1,0:T(8,128)(2,1)} %param.31) | copy-start | bytes 64516
  52.3 5.8 %copy-start.6 = (bf16[3,14,2048]{2,1,0:T(8,128)(2,1)S(1)}, bf16[3,14,2048]{2,1,0:T(8,128)(2,1)}, u32[]{:S(2)}) copy-start(bf16[3,14,2048]{2,1,0:T(8,128)(2,1)} %param.30) | copy-start | bytes 516100
  52.3 5.9 %copy-start.30 = (f32[3,14,32]{2,1,0:T(8,128)S(1)}, f32[3,14,32]{2,1,0:T(8,128)}, u32[]{:S(2)}) copy-start(f32[3,14,32]{2,1,0:T(8,128)} %param.33) | copy-start | bytes 16132
  52.3 5.9 %copy-start.36 = (f32[32]{0:T(128)S(1)}, f32[32]{0:T(128)}, u32[]{:S(2)}) copy-start(f32[32]{0:T(128)} %param.39) | copy-start | bytes 388
  52.3 6.0 %copy-start.37 = (f32[32]{0:T(128)S(1)}, f32[32]{0:T(128)}, u32[]{:S(2)}) copy-start(f32[32]{0:T(128)} %param.40) | copy-start | bytes 388
  52.3 6.3 %copy-start.15 = (bf16[3,14,1024]{2,1,0:T(8,128)(2,1)S(1)}, bf16[3,14,1024]{2,1,0:T(8,128)(2,1)}, u32[]{:S(2)}) copy-start(bf16[3,14,1024]{2,1,0:T(8,128)(2,1)} %param.34) | copy-start | bytes 258052
  52.3 164.7 %all-to-all-start.2 = ((bf16[16,28,64,128]{3,2,1,0:T(8,128)(2,1)}), bf16[16,28,64,128]{3,2,1,0:T(8,128)(2,1)}, u32[]{:S(2)}, u32[]{:S(2)}) async-start(bf16[16,28,64,128]{3,2,1,0:T(8,128)(2,1)} %copy-done), calls=%async_computation.3 | async-start | bytes 14680064 | tf_op jit(solution)/shard_map/all_to_all | solution.py:286
  57.4 3.9 %copy-start.35 = (f32[4,256]{1,0:T(4,128)S(1)}, f32[4,256]{1,0:T(4,128)}, u32[]{:S(2)}) copy-start(f32[4,256]{1,0:T(4,128)} %param.38) | copy-start | bytes 12292
  57.4 4.4 %copy-start.31 = (bf16[3,14,256]{2,1,0:T(8,128)(2,1)S(1)}, bf16[3,14,256]{2,1,0:T(8,128)(2,1)}, u32[]{:S(2)}) copy-start(bf16[3,14,256]{2,1,0:T(8,128)(2,1)} %param.36) | copy-start | bytes 64516
  57.4 4.4 %copy-start.32 = (bf16[3,14,256]{2,1,0:T(8,128)(2,1)S(1)}, bf16[3,14,256]{2,1,0:T(8,128)(2,1)}, u32[]{:S(2)}) copy-start(bf16[3,14,256]{2,1,0:T(8,128)(2,1)} %param.35) | copy-start | bytes 64516
  57.4 5.0 %copy-start.25 = (f32[4,2048]{1,0:T(4,128)S(1)}, f32[4,2048]{1,0:T(4,128)}, u32[]{:S(2)}) copy-start(f32[4,2048]{1,0:T(4,128)} %param.37) | copy-start | bytes 98308
  57.4 47.8 %reduce-scatter.2.cloned.1.call-start = ((), (), s32[]{:S(2)}) async-start(), calls=%async_computation.4 | async-start | bytes 491520 | tf_op jit(solution)/shard_map/reduce_scatter | solution.py:277
  58.1 5.0 %copy-start.14 = (bf16[3,14,2048]{2,1,0:T(8,128)(2,1)S(1)}, bf16[3,14,2048]{2,1,0:T(8,128)(2,1)}, u32[]{:S(2)}) copy-start(bf16[3,14,2048]{2,1,0:T(8,128)(2,1)} %param.32) | copy-start | bytes 516100
  68.3 4.4 %copy-start.33 = (s32[14]{0:T(128)S(1)}, s32[14]{0:T(128)}, u32[]{:S(2)}) copy-start(s32[14]{0:T(128)} %get-tuple-element.85) | copy-start | bytes 172
  68.3 4.6 %copy-start.38 = (s32[12]{0:T(128)S(1)}, s32[12]{0:T(128)}, u32[]{:S(2)}) copy-start(s32[12]{0:T(128)} %and_select_fusion) | copy-start | bytes 148
  68.3 4.8 %copy-start.19 = (bf16[14,256]{1,0:T(8,128)(2,1)S(1)}, bf16[14,256]{1,0:T(8,128)(2,1)}, u32[]{:S(2)}) copy-start(bf16[14,256]{1,0:T(8,128)(2,1)} %get-tuple-element.130) | copy-start | bytes 21508
  68.3 4.8 %copy-start.20 = (bf16[14,256]{1,0:T(8,128)(2,1)S(1)}, bf16[14,256]{1,0:T(8,128)(2,1)}, u32[]{:S(2)}) copy-start(bf16[14,256]{1,0:T(8,128)(2,1)} %get-tuple-element.131) | copy-start | bytes 21508
  68.4 4.8 %copy-start.21 = (bf16[14,256]{1,0:T(8,128)(2,1)S(1)}, bf16[14,256]{1,0:T(8,128)(2,1)}, u32[]{:S(2)}) copy-start(bf16[14,256]{1,0:T(8,128)(2,1)} %get-tuple-element.144) | copy-start | bytes 21508
  68.4 4.8 %copy-start.22 = (bf16[14,256]{1,0:T(8,128)(2,1)S(1)}, bf16[14,256]{1,0:T(8,128)(2,1)}, u32[]{:S(2)}) copy-start(bf16[14,256]{1,0:T(8,128)(2,1)} %get-tuple-element.145) | copy-start | bytes 21508
  68.4 4.8 %copy-start.23 = (bf16[14,256]{1,0:T(8,128)(2,1)S(1)}, bf16[14,256]{1,0:T(8,128)(2,1)}, u32[]{:S(2)}) copy-start(bf16[14,256]{1,0:T(8,128)(2,1)} %get-tuple-element.146) | copy-start | bytes 21508
  74.4 8.5 %copy-start.7 = (bf16[14,64,256]{2,1,0:T(8,128)(2,1)}, bf16[14,64,256]{2,1,0:T(8,128)(2,1)S(1)}, u32[]{:S(2)}) copy-start(bf16[14,64,256]{2,1,0:T(8,128)(2,1)S(1)} %get-tuple-element.157) | copy-start | bytes 1376260
  77.1 5.9 %copy-start.13 = (f32[3,14,256]{2,0,1:T(4,128)S(1)}, f32[3,14,256]{2,0,1:T(4,128)}, u32[]{:S(2)}) copy-start(f32[3,14,256]{2,0,1:T(4,128)} %copy-done.12) | copy-start | bytes 129028
  77.1 6.0 %copy-start.26 = (f32[1,2048]{1,0:T(1,128)S(1)}, f32[1,2048]{1,0:T(1,128)}, u32[]{:S(2)}) copy-start(f32[1,2048]{1,0:T(1,128)} %get-tuple-element.113) | copy-start | bytes 24580
  77.1 6.0 %copy-start.27 = (f32[1,2048]{1,0:T(1,128)S(1)}, f32[1,2048]{1,0:T(1,128)}, u32[]{:S(2)}) copy-start(f32[1,2048]{1,0:T(1,128)} %get-tuple-element.114) | copy-start | bytes 24580
  77.1 6.0 %copy-start.28 = (f32[1,2048]{1,0:T(1,128)S(1)}, f32[1,2048]{1,0:T(1,128)}, u32[]{:S(2)}) copy-start(f32[1,2048]{1,0:T(1,128)} %get-tuple-element.115) | copy-start | bytes 24580
  77.1 6.0 %copy-start.29 = (f32[1,2048]{1,0:T(1,128)S(1)}, f32[1,2048]{1,0:T(1,128)}, u32[]{:S(2)}) copy-start(f32[1,2048]{1,0:T(1,128)} %get-tuple-element.116) | copy-start | bytes 24580
  77.1 6.8 %copy-start.10 = (f32[14,1,2048]{2,1,0:T(1,128)S(1)}, f32[14,1,2048]{2,1,0:T(1,128)}, u32[]{:S(2)}) copy-start(f32[14,1,2048]{2,1,0:T(1,128)} %reshape.313) | copy-start | bytes 344068
  77.1 6.8 %copy-start.11 = (f32[14,1,2048]{2,1,0:T(1,128)S(1)}, f32[14,1,2048]{2,1,0:T(1,128)}, u32[]{:S(2)}) copy-start(f32[14,1,2048]{2,1,0:T(1,128)} %reshape.314) | copy-start | bytes 344068
  217.1 29.5 %all-to-all-start.1 = ((bf16[16,4,64,128]{3,2,1,0:T(8,128)(2,1)}), bf16[16,4,64,128]{3,2,1,0:T(8,128)(2,1)S(1)}, u32[]{:S(2)}, u32[]{:S(2)}) async-start(bf16[16,4,64,128]{3,2,1,0:T(8,128)(2,1)} %get-tuple-element.35), calls=%async_computation.2 | async-start | bytes 2097152 | tf_op jit(solution)/shard_map/all_to_all | solution.py:286
  (11 other events, 23.2 us)
Sparse Core Ops, SparseCore 0:
  83.1 22.1 reduce-scatter.1
